TPU v7x, 128 devices: a whole 4x4x4 slice. The times are simulated.
128 devices in a mesh: row: 8 (over y_hi, x), col: 16 (over y_lo, z, core).
Axes of the slice: x: 4, y: 4 (y_hi: 2, y_lo: 2; y = y_hi * 2 + y_lo), z: 4, core: 2. Of those that a mesh axis runs over, the one named last changes fastest.
Arguments:
- homolog_features: bfloat16 [1024, 1024, 256], P(('row', 'col')), may hold values from -8 to 8
- presence_flags: int32 [1024, 1024], P(('row', 'col')), may hold values from 0 to 1, as said below
- residue_chain_index: int32 [1024], replicated, may hold values from 0 to 3, never falling along the last dimension, each value on 1 to 512 neighbouring positions
- pair_state: bfloat16 [1024, 1024, 128], P('row', 'col'), may hold values from -6 to 6
- standardize_scale: float32 [256], replicated, may hold values from 0.1 to 1.9
- standardize_shift: float32 [256], replicated, may hold values from -3 to 3
- left_factor_matrix: bfloat16 [256, 32], replicated, may hold values from -0.375 to 0.375
- right_factor_matrix: bfloat16 [256, 32], replicated, may hold values from -0.375 to 0.375
- output_weight: bfloat16 [1024, 128], replicated, may hold values from -0.1875 to 0.1875
- chain_pair_bias: float32 [2, 128], replicated, may hold values from -3 to 3
Outputs:
- pair_out: bfloat16 [1024, 1024, 128], P('row', 'col')
Inputs may be any that keep to these rules, and one draw needn't show every extreme that they name: `presence_flags`: entries are 0 or 1; sequence 0, the query, is 1 at every residue. `residue_chain_index`: chain numbers never fall along the residues.
All inputs are finite; a program needn't handle non-finite values.
Results may differ from a plain program's by a relative error of at most 0.0036.
Values may be sent and summed in bfloat16 or wider, within the bound.
A program may use at most 128 MiB of HBM per device.

v0:
```python
import math

import jax
import jax.numpy as jnp
from jax import lax
from jax.sharding import PartitionSpec as P


def standardize_features(homolog_features, standardize_scale, standardize_shift):
    value_rows = homolog_features.astype(jnp.float32)
    centre = jnp.mean(value_rows, axis=-1, keepdims=True)
    variance = jnp.mean(jnp.square(value_rows - centre), axis=-1, keepdims=True)
    return (
        (value_rows - centre) * lax.rsqrt(variance + 1e-05) * standardize_scale + standardize_shift
    ).astype(jnp.bfloat16)


def pair_terms(rows_left, rows_mask, cols_right, cols_mask, out_matrix):
    row_count, outer_width, seq_total = rows_left.shape
    col_count = cols_right.shape[0]
    sub_rows = math.gcd(row_count, 16)
    flat_right = cols_right.reshape(col_count * outer_width, seq_total)

    def one_block(parts):
        left_block, mask_block = parts
        outer_prod = lax.dot_general(
            left_block.reshape(sub_rows * outer_width, seq_total),
            flat_right,
            (((1,), (1,)), ((), ())),
            preferred_element_type=jnp.float32,
        )
        outer_prod = outer_prod.astype(jnp.bfloat16).reshape(
            sub_rows, outer_width, col_count, outer_width
        )
        update = jnp.einsum(
            "icje,cez->ijz", outer_prod, out_matrix, preferred_element_type=jnp.float32
        )
        counts = lax.dot_general(
            mask_block, cols_mask, (((1,), (1,)), ((), ())), preferred_element_type=jnp.float32
        )
        return update / (counts[:, :, None] + 0.001)

    blocks = lax.map(
        one_block,
        (
            rows_left.reshape(row_count // sub_rows, sub_rows, outer_width, seq_total),
            rows_mask.reshape(row_count // sub_rows, sub_rows, seq_total),
        ),
    )
    return blocks.reshape(row_count, col_count, -1)


def per_device(
    homolog_features,
    presence_flags,
    residue_chain_index,
    pair_state,
    standardize_scale,
    standardize_shift,
    left_factor_matrix,
    right_factor_matrix,
    output_weight,
    chain_pair_bias,
):
    local_sequences, residue_count, channel_count = homolog_features.shape
    outer_width = left_factor_matrix.shape[1]
    rows_axis = lax.axis_size("row")
    cols_axis = lax.axis_size("col")
    devices = rows_axis * cols_axis
    share_len = residue_count // devices
    standardized_homologs = standardize_features(
        homolog_features, standardize_scale, standardize_shift
    ).reshape(local_sequences * residue_count, channel_count)
    presence_real = presence_flags.astype(jnp.float32)
    projected = jnp.dot(
        standardized_homologs,
        jnp.concatenate([left_factor_matrix, right_factor_matrix], axis=1),
        preferred_element_type=jnp.float32,
    )
    projected = (
        projected.reshape(local_sequences, residue_count, 2 * outer_width)
        * presence_real[:, :, None]
    ).astype(jnp.bfloat16)
    first_factor_vectors = projected[:, :, :outer_width].reshape(
        local_sequences, devices, share_len, outer_width
    )
    second_factor_vectors = projected[:, :, outer_width:].reshape(
        local_sequences, cols_axis, rows_axis, share_len, outer_width
    )
    second_factor_vectors = jnp.transpose(second_factor_vectors, (0, 2, 1, 3, 4)).reshape(
        local_sequences, devices, share_len, outer_width
    )
    send_values = jnp.transpose(
        jnp.concatenate([first_factor_vectors, second_factor_vectors], axis=3), (1, 2, 3, 0)
    ).reshape(devices, -1)
    half_mask = presence_flags.astype(jnp.bfloat16)
    left_mask = half_mask.reshape(local_sequences, devices, share_len)
    right_mask = jnp.transpose(
        half_mask.reshape(local_sequences, cols_axis, rows_axis, share_len), (0, 2, 1, 3)
    ).reshape(local_sequences, devices, share_len)
    send_mask = jnp.transpose(jnp.stack([left_mask, right_mask], axis=3), (1, 2, 3, 0)).reshape(
        devices, -1
    )
    got_values, got_mask = (
        lax.all_to_all(send_values, ("row", "col"), split_axis=0, concat_axis=0, tiled=True),
        lax.all_to_all(send_mask, ("row", "col"), split_axis=0, concat_axis=0, tiled=True),
    )
    got_values = jnp.transpose(
        got_values.reshape(devices, share_len, 2 * outer_width, local_sequences), (1, 2, 0, 3)
    ).reshape(share_len, 2 * outer_width, devices * local_sequences)
    left_part = got_values[:, :outer_width]
    right_part = got_values[:, outer_width:]
    got_mask = jnp.transpose(
        got_mask.reshape(devices, share_len, 2, local_sequences), (1, 2, 0, 3)
    ).reshape(share_len, 2, devices * local_sequences)
    left_mpart = got_mask[:, 0]
    right_mpart = got_mask[:, 1]
    rows_len = residue_count // rows_axis
    cols_len = residue_count // cols_axis
    row_chain = lax.dynamic_slice_in_dim(
        residue_chain_index, lax.axis_index("row") * rows_len, rows_len, 0
    )
    col_chain = lax.dynamic_slice_in_dim(
        residue_chain_index, lax.axis_index("col") * cols_len, cols_len, 0
    )
    same_chain = (row_chain[:, None] == col_chain[None, :])[:, :, None]
    base_pair = pair_state.astype(jnp.float32) + jnp.where(
        same_chain, chain_pair_bias[0], chain_pair_bias[1]
    )
    out_matrix = output_weight.reshape(outer_width, outer_width, -1)
    rows_left, rows_mask = (
        lax.all_gather(left_part, "col", axis=0, tiled=True),
        lax.all_gather(left_mpart, "col", axis=0, tiled=True),
    )
    cols_right = lax.all_gather(right_part, "row", axis=0, tiled=True)
    cols_mask = lax.all_gather(right_mpart, "row", axis=0, tiled=True)
    update = pair_terms(rows_left, rows_mask, cols_right, cols_mask, out_matrix)
    result = base_pair + update
    return result.astype(jnp.bfloat16)


def solution(mesh):
    return jax.shard_map(
        per_device,
        mesh=mesh,
        in_specs=(
            P(("row", "col"), None, None),
            P(("row", "col"), None),
            P(),
            P("row", "col", None),
            P(),
            P(),
            P(),
            P(),
            P(),
            P(),
        ),
        out_specs=P("row", "col", None),
        check_vma=False,
    )
```

profile of v0, /device:TPU:1, one launch (start us, length us, event | category | flops | bytes accessed | tf_op | source)
XLA Modules:
  0.0 367.2 jit_solution(11927189536988325662)
XLA Ops:
  6.6 3.5 convert_reduce_fusion
  10.1 2.4 fusion.9
  12.7 4.0 %multiply_convert_fusion = bf16[8,1024,64]{1,2,0:T(8,128)(2,1)S(1)} fusion(bf16[8,1024,256]{2,1,0:T(8,128)(2,1)S(1)} %copy-done, f32[256]{0:T(256)S(1)} %copy-done.7, f32[256]{0:T(256)S(1)} %copy-done.8, f32[8,1024]{1,0:T(8,128)S(1)} %add_rsqrt_fusion, f32[8,1024]{1,0:T(8,128)S(1)} %broadcast_multiply_fusion, f32[8,1024]{1,0:T(8,128)S(1)} %get-tuple-element.78, ...), kind=kOutput, calls=%fused_computation.23 | convolution fusion | flops 282132480 | bytes 5376000 | tf_op jit(solution)/shard_map/dot_general | solution.py:75
  17.8 1.9 copy.55
  20.7 4.1 %maximum_bitcast_fusion = bf16[128,8,64,8]{2,1,0,3:T(8,128)(2,1)} fusion(bf16[8,128,8,32]{3,2,1,0:T(8,128)(2,1)} %bitcast.85, bf16[8,128,8,32]{3,2,1,0:T(8,128)(2,1)S(1)} %bitcast.84), kind=kLoop, calls=%fused_computation.22 | loop fusion | flops 2097152 | bytes 2097152 | tf_op jit(solution)/shard_map/transpose | solution.py:93
  24.8 3.2 copy.56
  28.5 1.4 reduce
  31.3 30.9 %all_to_all.18 = bf16[128,2,2048]{2,1,0:T(2,128)(2,1)S(1)} all-to-all(bf16[128,2,2048]{2,1,0:T(2,128)(2,1)S(1)} %reshape.123), channel_id=1, replica_groups=mesh['row'=8,'col'=16] {'row','col'}, dimensions={0} | all-to-all | bytes 2097152 | tf_op jit(solution)/shard_map/all_to_all | solution.py:105
  63.3 2.6 copy.58
  65.9 1.4 copy.59
  67.3 2.8 fusion.21
  70.1 2.7 copy.61
  73.1 1.5 copy.60
  76.5 3.7 %all-to-all-start.1 = ((bf16[128,1,128]{2,1,0:T(2,128)(2,1)}), bf16[128,1,128]{2,1,0:T(2,128)(2,1)S(1)}, u32[]{:S(2)}, u32[]{:S(2)}) async-start(bf16[128,1,128]{2,1,0:T(2,128)(2,1)} %copy.65), calls=%async_computation.1 | async-start | bytes 131072 | tf_op jit(solution)/shard_map/all_to_all | solution.py:106
  81.8 8.4 %all-to-all-done.1 = bf16[128,1,128]{2,1,0:T(2,128)(2,1)S(1)} async-done(((bf16[128,1,128]{2,1,0:T(2,128)(2,1)}), bf16[128,1,128]{2,1,0:T(2,128)(2,1)S(1)}, u32[]{:S(2)}, u32[]{:S(2)}) %all-to-all-start.1) | async-done | bytes 32800 | tf_op jit(solution)/shard_map/all_to_all | solution.py:106
  91.4 28.1 %all-gather.1 = bf16[64,1,1024]{2,0,1:T(8,128)(2,1)S(1)} all-gather(bf16[8,1,1024]{2,0,1:T(8,128)(2,1)S(1)} %get-tuple-element.75), channel_id=3, replica_groups=mesh['row'=8,'col'=16] {'row'}, dimensions={0}, use_global_device_ids=true | all-gather | bytes 147456 | tf_op jit(solution)/shard_map/all_gather | solution.py:136
  119.5 24.5 %all-gather = bf16[128,1,1024]{2,0,1:T(8,128)(2,1)S(1)} all-gather(bf16[8,1,1024]{2,0,1:T(8,128)(2,1)S(1)} %get-tuple-element.76), channel_id=2, replica_groups=mesh['row'=8,'col'=16] {'col'}, dimensions={0}, use_global_device_ids=true | all-gather | bytes 278528 | tf_op jit(solution)/shard_map/all_gather | solution.py:133
  144.0 49.6 %all-gather.5.cloned.1.call-done = bf16[128,32,1024]{2,1,0:T(8,128)(2,1)} async-done(((bf16[8,32,1024]{2,1,0:T(8,128)(2,1)}), bf16[128,32,1024]{2,1,0:T(8,128)(2,1)}) %all-gather.5.cloned.1.call-update) | async-done | bytes 8388624 | tf_op jit(solution)/shard_map/all_gather | solution.py:132
  193.6 160.7 %while.10 = (s32[]{:T(128)}, f32[8,16,64,128]{3,2,1,0:T(8,128)}, bf16[8,16,32,1024]{3,2,1,0:T(8,128)(2,1)}, bf16[2048,1024]{1,0:T(8,128)(2,1)}, bf16[32,32,128]{...) while((s32[]{:T(128)}, f32[8,16,64,128]{3,2,1,0:T(8,128)}, ...), condition=%wide.region_3.4_spmd, body=%wide.region_2.3_spmd.sunk | while | flops 2419196928 | bytes 22979164 | solution.py:43
  193.6 1.3 constant_dynamic-slice_fusion.2
  194.9 4.6 %convolution_convert_fusion.2 = bf16[512,2048]{1,0:T(8,128)(2,1)S(1)} fusion(bf16[512,1024]{1,0:T(8,128)(2,1)S(1)} %bitcast.82, bf16[2048,1024]{1,0:T(8,128)(2,1)} %get-tuple-element.143), kind=kOutput, calls=%fused_computation.clone.1 | convolution fusion | flops 2148532224 | bytes 7340032 | tf_op jit(solution)/shard_map/while/body/eval_jaxpr/dot_general | solution.py:26
  199.5 8.1 %reshape.126 = bf16[16,32,64,32]{3,2,1,0:T(8,128)(2,1)} reshape(bf16[512,2048]{1,0:T(8,128)(2,1)S(1)} %convolution_convert_fusion.2) | data formatting | bytes 4194304 | tf_op jit(solution)/shard_map/while/body/eval_jaxpr/reshape | solution.py:32
  207.7 5.9 %fusion.42 = f32[8,16,64,128]{3,2,1,0:T(8,128)} fusion(f32[8,16,64,128]{3,2,1,0:T(8,128)} %get-tuple-element.133, s32[]{:T(128)} %get-tuple-element.132, bf16[16,32,64,32]{3,2,1,0:T(8,128)(2,1)} %reshape.126, bf16[32,32,128]{2,1,0:T(8,128)(2,1)S(1)} %get-tuple-element.144, f32[16,64]{1,0:T(8,128)S(1)} %convolution_add_fusion.2), kind=kOutput, calls=%fused_computation.4.clone.1 | convolution fusion | flops 268566528 | bytes 9179648 | tf_op jit(solution)/shard_map/while/body/eval_jaxpr/icje,cez->ijz/dot_general | solution.py:35
  213.7 1.3 constant_dynamic-slice_fusion.2
  215.0 4.6 %convolution_convert_fusion.2 = bf16[512,2048]{1,0:T(8,128)(2,1)S(1)} fusion(bf16[512,1024]{1,0:T(8,128)(2,1)S(1)} %bitcast.82, bf16[2048,1024]{1,0:T(8,128)(2,1)} %get-tuple-element.143), kind=kOutput, calls=%fused_computation.clone.1 | convolution fusion | flops 2148532224 | bytes 7340032 | tf_op jit(solution)/shard_map/while/body/eval_jaxpr/dot_general | solution.py:26
  219.6 8.1 %reshape.126 = bf16[16,32,64,32]{3,2,1,0:T(8,128)(2,1)} reshape(bf16[512,2048]{1,0:T(8,128)(2,1)S(1)} %convolution_convert_fusion.2) | data formatting | bytes 4194304 | tf_op jit(solution)/shard_map/while/body/eval_jaxpr/reshape | solution.py:32
  227.8 5.9 %fusion.42 = f32[8,16,64,128]{3,2,1,0:T(8,128)} fusion(f32[8,16,64,128]{3,2,1,0:T(8,128)} %get-tuple-element.133, s32[]{:T(128)} %get-tuple-element.132, bf16[16,32,64,32]{3,2,1,0:T(8,128)(2,1)} %reshape.126, bf16[32,32,128]{2,1,0:T(8,128)(2,1)S(1)} %get-tuple-element.144, f32[16,64]{1,0:T(8,128)S(1)} %convolution_add_fusion.2), kind=kOutput, calls=%fused_computation.4.clone.1 | convolution fusion | flops 268566528 | bytes 9179648 | tf_op jit(solution)/shard_map/while/body/eval_jaxpr/icje,cez->ijz/dot_general | solution.py:35
  233.7 1.3 constant_dynamic-slice_fusion.2
  235.1 4.6 %convolution_convert_fusion.2 = bf16[512,2048]{1,0:T(8,128)(2,1)S(1)} fusion(bf16[512,1024]{1,0:T(8,128)(2,1)S(1)} %bitcast.82, bf16[2048,1024]{1,0:T(8,128)(2,1)} %get-tuple-element.143), kind=kOutput, calls=%fused_computation.clone.1 | convolution fusion | flops 2148532224 | bytes 7340032 | tf_op jit(solution)/shard_map/while/body/eval_jaxpr/dot_general | solution.py:26
  239.6 8.1 %reshape.126 = bf16[16,32,64,32]{3,2,1,0:T(8,128)(2,1)} reshape(bf16[512,2048]{1,0:T(8,128)(2,1)S(1)} %convolution_convert_fusion.2) | data formatting | bytes 4194304 | tf_op jit(solution)/shard_map/while/body/eval_jaxpr/reshape | solution.py:32
  247.9 6.0 %fusion.42 = f32[8,16,64,128]{3,2,1,0:T(8,128)} fusion(f32[8,16,64,128]{3,2,1,0:T(8,128)} %get-tuple-element.133, s32[]{:T(128)} %get-tuple-element.132, bf16[16,32,64,32]{3,2,1,0:T(8,128)(2,1)} %reshape.126, bf16[32,32,128]{2,1,0:T(8,128)(2,1)S(1)} %get-tuple-element.144, f32[16,64]{1,0:T(8,128)S(1)} %convolution_add_fusion.2), kind=kOutput, calls=%fused_computation.4.clone.1 | convolution fusion | flops 268566528 | bytes 9179648 | tf_op jit(solution)/shard_map/while/body/eval_jaxpr/icje,cez->ijz/dot_general | solution.py:35
  253.9 1.3 constant_dynamic-slice_fusion.2
  255.2 4.6 %convolution_convert_fusion.2 = bf16[512,2048]{1,0:T(8,128)(2,1)S(1)} fusion(bf16[512,1024]{1,0:T(8,128)(2,1)S(1)} %bitcast.82, bf16[2048,1024]{1,0:T(8,128)(2,1)} %get-tuple-element.143), kind=kOutput, calls=%fused_computation.clone.1 | convolution fusion | flops 2148532224 | bytes 7340032 | tf_op jit(solution)/shard_map/while/body/eval_jaxpr/dot_general | solution.py:26
  259.7 8.1 %reshape.126 = bf16[16,32,64,32]{3,2,1,0:T(8,128)(2,1)} reshape(bf16[512,2048]{1,0:T(8,128)(2,1)S(1)} %convolution_convert_fusion.2) | data formatting | bytes 4194304 | tf_op jit(solution)/shard_map/while/body/eval_jaxpr/reshape | solution.py:32
  268.0 5.9 %fusion.42 = f32[8,16,64,128]{3,2,1,0:T(8,128)} fusion(f32[8,16,64,128]{3,2,1,0:T(8,128)} %get-tuple-element.133, s32[]{:T(128)} %get-tuple-element.132, bf16[16,32,64,32]{3,2,1,0:T(8,128)(2,1)} %reshape.126, bf16[32,32,128]{2,1,0:T(8,128)(2,1)S(1)} %get-tuple-element.144, f32[16,64]{1,0:T(8,128)S(1)} %convolution_add_fusion.2), kind=kOutput, calls=%fused_computation.4.clone.1 | convolution fusion | flops 268566528 | bytes 9179648 | tf_op jit(solution)/shard_map/while/body/eval_jaxpr/icje,cez->ijz/dot_general | solution.py:35
  275.3 4.6 %convolution_convert_fusion.2 = bf16[512,2048]{1,0:T(8,128)(2,1)S(1)} fusion(bf16[512,1024]{1,0:T(8,128)(2,1)S(1)} %bitcast.82, bf16[2048,1024]{1,0:T(8,128)(2,1)} %get-tuple-element.143), kind=kOutput, calls=%fused_computation.clone.1 | convolution fusion | flops 2148532224 | bytes 7340032 | tf_op jit(solution)/shard_map/while/body/eval_jaxpr/dot_general | solution.py:26
  279.8 8.1 %reshape.126 = bf16[16,32,64,32]{3,2,1,0:T(8,128)(2,1)} reshape(bf16[512,2048]{1,0:T(8,128)(2,1)S(1)} %convolution_convert_fusion.2) | data formatting | bytes 4194304 | tf_op jit(solution)/shard_map/while/body/eval_jaxpr/reshape | solution.py:32
  288.1 5.9 %fusion.42 = f32[8,16,64,128]{3,2,1,0:T(8,128)} fusion(f32[8,16,64,128]{3,2,1,0:T(8,128)} %get-tuple-element.133, s32[]{:T(128)} %get-tuple-element.132, bf16[16,32,64,32]{3,2,1,0:T(8,128)(2,1)} %reshape.126, bf16[32,32,128]{2,1,0:T(8,128)(2,1)S(1)} %get-tuple-element.144, f32[16,64]{1,0:T(8,128)S(1)} %convolution_add_fusion.2), kind=kOutput, calls=%fused_computation.4.clone.1 | convolution fusion | flops 268566528 | bytes 9179648 | tf_op jit(solution)/shard_map/while/body/eval_jaxpr/icje,cez->ijz/dot_general | solution.py:35
  295.3 4.6 %convolution_convert_fusion.2 = bf16[512,2048]{1,0:T(8,128)(2,1)S(1)} fusion(bf16[512,1024]{1,0:T(8,128)(2,1)S(1)} %bitcast.82, bf16[2048,1024]{1,0:T(8,128)(2,1)} %get-tuple-element.143), kind=kOutput, calls=%fused_computation.clone.1 | convolution fusion | flops 2148532224 | bytes 7340032 | tf_op jit(solution)/shard_map/while/body/eval_jaxpr/dot_general | solution.py:26
  299.9 8.1 %reshape.126 = bf16[16,32,64,32]{3,2,1,0:T(8,128)(2,1)} reshape(bf16[512,2048]{1,0:T(8,128)(2,1)S(1)} %convolution_convert_fusion.2) | data formatting | bytes 4194304 | tf_op jit(solution)/shard_map/while/body/eval_jaxpr/reshape | solution.py:32
  308.2 5.9 %fusion.42 = f32[8,16,64,128]{3,2,1,0:T(8,128)} fusion(f32[8,16,64,128]{3,2,1,0:T(8,128)} %get-tuple-element.133, s32[]{:T(128)} %get-tuple-element.132, bf16[16,32,64,32]{3,2,1,0:T(8,128)(2,1)} %reshape.126, bf16[32,32,128]{2,1,0:T(8,128)(2,1)S(1)} %get-tuple-element.144, f32[16,64]{1,0:T(8,128)S(1)} %convolution_add_fusion.2), kind=kOutput, calls=%fused_computation.4.clone.1 | convolution fusion | flops 268566528 | bytes 9179648 | tf_op jit(solution)/shard_map/while/body/eval_jaxpr/icje,cez->ijz/dot_general | solution.py:35
  315.4 4.6 %convolution_convert_fusion.2 = bf16[512,2048]{1,0:T(8,128)(2,1)S(1)} fusion(bf16[512,1024]{1,0:T(8,128)(2,1)S(1)} %bitcast.82, bf16[2048,1024]{1,0:T(8,128)(2,1)} %get-tuple-element.143), kind=kOutput, calls=%fused_computation.clone.1 | convolution fusion | flops 2148532224 | bytes 7340032 | tf_op jit(solution)/shard_map/while/body/eval_jaxpr/dot_general | solution.py:26
  320.0 8.1 %reshape.126 = bf16[16,32,64,32]{3,2,1,0:T(8,128)(2,1)} reshape(bf16[512,2048]{1,0:T(8,128)(2,1)S(1)} %convolution_convert_fusion.2) | data formatting | bytes 4194304 | tf_op jit(solution)/shard_map/while/body/eval_jaxpr/reshape | solution.py:32
  328.2 5.9 %fusion.42 = f32[8,16,64,128]{3,2,1,0:T(8,128)} fusion(f32[8,16,64,128]{3,2,1,0:T(8,128)} %get-tuple-element.133, s32[]{:T(128)} %get-tuple-element.132, bf16[16,32,64,32]{3,2,1,0:T(8,128)(2,1)} %reshape.126, bf16[32,32,128]{2,1,0:T(8,128)(2,1)S(1)} %get-tuple-element.144, f32[16,64]{1,0:T(8,128)S(1)} %convolution_add_fusion.2), kind=kOutput, calls=%fused_computation.4.clone.1 | convolution fusion | flops 268566528 | bytes 9179648 | tf_op jit(solution)/shard_map/while/body/eval_jaxpr/icje,cez->ijz/dot_general | solution.py:35
  335.5 4.6 %convolution_convert_fusion.2 = bf16[512,2048]{1,0:T(8,128)(2,1)S(1)} fusion(bf16[512,1024]{1,0:T(8,128)(2,1)S(1)} %bitcast.82, bf16[2048,1024]{1,0:T(8,128)(2,1)} %get-tuple-element.143), kind=kOutput, calls=%fused_computation.clone.1 | convolution fusion | flops 2148532224 | bytes 7340032 | tf_op jit(solution)/shard_map/while/body/eval_jaxpr/dot_general | solution.py:26
  340.0 8.1 %reshape.126 = bf16[16,32,64,32]{3,2,1,0:T(8,128)(2,1)} reshape(bf16[512,2048]{1,0:T(8,128)(2,1)S(1)} %convolution_convert_fusion.2) | data formatting | bytes 4194304 | tf_op jit(solution)/shard_map/while/body/eval_jaxpr/reshape | solution.py:32
  348.3 6.0 %fusion.42 = f32[8,16,64,128]{3,2,1,0:T(8,128)} fusion(f32[8,16,64,128]{3,2,1,0:T(8,128)} %get-tuple-element.133, s32[]{:T(128)} %get-tuple-element.132, bf16[16,32,64,32]{3,2,1,0:T(8,128)(2,1)} %reshape.126, bf16[32,32,128]{2,1,0:T(8,128)(2,1)S(1)} %get-tuple-element.144, f32[16,64]{1,0:T(8,128)S(1)} %convolution_add_fusion.2), kind=kOutput, calls=%fused_computation.4.clone.1 | convolution fusion | flops 268566528 | bytes 9179648 | tf_op jit(solution)/shard_map/while/body/eval_jaxpr/icje,cez->ijz/dot_general | solution.py:35
  354.3 6.1 %fusion.13 = bf16[128,64,128]{2,1,0:T(8,128)(2,1)} fusion(f32[8,16,64,128]{3,2,1,0:T(8,128)} %get-tuple-element.42, bf16[128,64,128]{2,1,0:T(8,128)(2,1)} %param.15, f32[128]{0:T(128)S(1)} %get-tuple-element.80, f32[128]{0:T(128)S(1)} %get-tuple-element.79, pred[128,64]{1,0:T(8,128)(4,1)S(1)} %broadcast_compare_fusion), kind=kLoop, calls=%fused_computation.20 | loop fusion | flops 5242880 | bytes 8397824 | tf_op jit(solution)/shard_map/convert_element_type | solution.py:139
  (60 shorter events, 16.3 us)
Async XLA Ops:
  6.5 6.1 %copy-start.2 = (s32[8,1024]{1,0:T(8,128)S(1)}, s32[8,1024]{1,0:T(8,128)}, u32[]{:S(2)}) copy-start(s32[8,1024]{1,0:T(8,128)} %param.13) | copy-start | bytes 98308
  6.5 6.1 %copy-start.8 = (f32[256]{0:T(256)S(1)}, f32[256]{0:T(256)}, u32[]{:S(2)}) copy-start(f32[256]{0:T(256)} %param.16) | copy-start | bytes 3076
  6.5 6.1 %copy-start.7 = (f32[256]{0:T(256)S(1)}, f32[256]{0:T(256)}, u32[]{:S(2)}) copy-start(f32[256]{0:T(256)} %param.17) | copy-start | bytes 3076
  6.5 6.1 %copy-start.6 = (bf16[256,32]{0,1:T(8,128)(2,1)S(1)}, bf16[256,32]{0,1:T(8,128)(2,1)}, u32[]{:S(2)}) copy-start(bf16[256,32]{0,1:T(8,128)(2,1)} %param.18) | copy-start | bytes 49156
  6.5 6.1 %copy-start.5 = (bf16[256,32]{0,1:T(8,128)(2,1)S(1)}, bf16[256,32]{0,1:T(8,128)(2,1)}, u32[]{:S(2)}) copy-start(bf16[256,32]{0,1:T(8,128)(2,1)} %param.19) | copy-start | bytes 49156
  6.5 137.4 %all-gather.7.cloned.1.call-start = ((), (), s32[]{:S(2)}) async-start(), calls=%async_computation.3 | async-start | bytes 4718592 | tf_op jit(solution)/shard_map/all_gather | solution.py:135
  6.6 3.5 copy-start
  70.1 3.0 copy-start.1
  70.1 11.7 %copy-start.3 = (f32[2,128]{1,0:T(2,128)S(1)}, f32[2,128]{1,0:T(2,128)}, u32[]{:S(2)}) copy-start(f32[2,128]{1,0:T(2,128)} %param.21) | copy-start | bytes 3076
  72.8 120.8 %copy-start.4 = (bf16[1024,128]{1,0:T(8,128)(2,1)S(1)}, bf16[1024,128]{1,0:T(8,128)(2,1)}, u32[]{:S(2)}) copy-start(bf16[1024,128]{1,0:T(8,128)(2,1)} %param.20) | copy-start | bytes 786436
  72.9 120.7 %all-gather.5.cloned.1.call-start = ((), (), s32[]{:S(2)}) async-start(), calls=%async_computation.2 | async-start | bytes 8912896 | tf_op jit(solution)/shard_map/all_gather | solution.py:132
  76.5 13.8 %all-to-all-start.1 = ((bf16[128,1,128]{2,1,0:T(2,128)(2,1)}), bf16[128,1,128]{2,1,0:T(2,128)(2,1)S(1)}, u32[]{:S(2)}, u32[]{:S(2)}) async-start(bf16[128,1,128]{2,1,0:T(2,128)(2,1)} %copy.65), calls=%async_computation.1 | async-start | bytes 131072 | tf_op jit(solution)/shard_map/all_to_all | solution.py:106
Sparse Core Ops, SparseCore 0:
  73.0 68.2 all-gather.6
  143.0 50.5 all-gather.4
where the time goes:
time: 369 us; the launch traced here: 367 us
  local copies, waits for them, and re-layouts  101 us (27%)
  matrix products  89.1 us (24%)
  blocking collectives  83.5 us (23%)
  waiting for transfers between devices  58.1 us (16%)
  other arithmetic  17.8 us (5%)
  between operations  13.7 us (4%)
  starting transfers between devices  3.96 us (1%)
    reshape x8, local copies, waits for them, and re-layouts, one_block(): outer_prod.astype(jnp.bfloat16)  64.9 us
    all_gather x1, waiting for transfers between devices, per_device(): lax.all_gather(left_part, 'col', axis=0, tiled=True)  49.6 us
    dot_general x8, matrix products, one_block(): jnp.einsum('icje,cez->ijz', outer_prod, out_matrix, preferred_element_typ...  47.5 us
    dot_general x8, matrix products, one_block(): lax.dot_general(left_block.reshape(sub_rows * outer_width, seq_total), fl...  36.4 us
    all_to_all x1, blocking collectives, per_device(): lax.all_to_all(send_values, ('row', 'col'), split_axis=0, concat_axis=0,...  30.9 us
    all_gather x1, blocking collectives, per_device(): cols_mask = lax.all_gather(right_mpart, 'row', axis=0, tiled=True)  28.1 us
    all_gather x1, blocking collectives, per_device(): lax.all_gather(left_mpart, 'col', axis=0, tiled=True)  24.5 us
    dynamic_slice x8, local copies, waits for them, and re-layouts, pair_terms(): lax.map(one_block, (rows_left.reshape(row_count // sub_rows, sub_rows, ou...  10.5 us
  transfers between devices with their start and end apart: 3, of which 2 were waited for; matrix products, arithmetic and copies ran while one was open for 2% of the time, Pallas kernels for 0%

commit v1 on v0

v1 whole, which is shorter than its diff:
```python
import jax
import jax.numpy as jnp
from jax import lax
from jax.experimental import pallas as pl
from jax.experimental.pallas import tpu as pltpu
from jax.sharding import PartitionSpec as P

MESH = pl.DeviceIdType.MESH
F32 = jnp.float32
BF16 = jnp.bfloat16
Q = 4
CJ = 16
NG = 2
MQ = 1


def kernel(
    feats, flags, chain_rows, chain_s, pair, scale, shift, wl, wr, wout, bias,
    out,
    F, Y, SB, RL, RR, L, Lm, R, SX, T, WT, PT, acc, CT, pair_v, out_v, bT,
    f_sem, p_sem, o_sem, a_ss, a_rl, a_rr, x_ss, x_rs, l_ss, l_rs, r_ss, r_rs,
):
    row = lax.axis_index("row")
    col = lax.axis_index("col")
    yh, x = row // 4, row % 4
    cc, core = col // 2, col % 2
    yl, z = cc // 4, cc % 4

    def dev(yh_, x_, yl_, z_, k_):
        return (yh_ * 4 + x_, yl_ * 8 + z_ * 2 + k_)

    def rc(src, dst, ss, rs, d):
        return pltpu.make_async_remote_copy(
            src_ref=src, dst_ref=dst, send_sem=ss, recv_sem=rs, device_id=d, device_id_type=MESH
        )

    bar = pltpu.get_barrier_semaphore()
    for n in range(8):
        for k in range(2):
            @pl.when(jnp.logical_not(jnp.logical_and(n == row, k == core)))
            def _():
                pl.semaphore_signal(bar, inc=1, device_id=(n, cc * 2 + k), device_id_type=MESH)
    for m in range(8):
        for k in range(2):
            @pl.when(m != cc)
            def _():
                pl.semaphore_signal(bar, inc=1, device_id=(row, m * 2 + k), device_id_type=MESH)

    def block_of(k):
        return lax.rem(row + cc + k, 8)

    def f_copy(k):
        b = block_of(k)
        return pltpu.make_async_copy(
            feats.at[:, pl.ds(pl.multiple_of(b * 128, 128), 128), :], F.at[k], f_sem.at[k]
        )

    for k in range(8):
        f_copy(k).start()
    p_copy = pltpu.make_async_copy(pair, pair_v, p_sem)
    p_copy.start()

    PT[...] = jnp.transpose(
        jnp.concatenate([wl[...].astype(F32), wr[...].astype(F32)], axis=1)
    ).astype(BF16)

    def project(k):
        b = block_of(k)
        present = flags[:, pl.ds(pl.multiple_of(b * 128, 128), 128)].astype(F32)
        for sp in range(4):
            v = F[k, 2 * sp:2 * sp + 2].reshape(256, 256).astype(F32)
            mu = jnp.mean(v, axis=-1, keepdims=True)
            d = v - mu
            var = jnp.mean(d * d, axis=-1, keepdims=True)
            nrm = (d * lax.rsqrt(var + 1e-05) * scale[...] + shift[...]).astype(BF16)
            pr = lax.dot_general(
                PT[...], nrm, (((1,), (1,)), ((), ())), preferred_element_type=F32
            )
            for u in range(2):
                s = 2 * sp + u
                Y[pl.ds(s, 64, stride=8), :] = pr[:, u * 128:(u + 1) * 128] * present[s:s + 1, :]
        pad = jnp.concatenate([present, jnp.zeros_like(present)], axis=0).astype(BF16)
        for h in range(2):
            for g in range(8):
                SB[b, h, 16 * g:16 * g + 16, :] = Y[(4 * g + 2 * h) * 8:(4 * g + 2 * h) * 8 + 16, :].astype(BF16)
            SB[b, 2 + h, 0:128, :] = Y[256 + h * 128:256 + (h + 1) * 128, :].astype(BF16)
            SB[b, h, 128:144, :] = pad
            SB[b, 2 + h, 128:144, :] = pad

    def scatter(k, wait):
        b = block_of(k)
        for h in range(2):
            mine = jnp.logical_and(b == row, h == core)
            left = rc(SB.at[b, h], RL.at[row, core], a_ss.at[k, h], a_rl.at[row, core], (b, cc * 2 + h))

            @pl.when(jnp.logical_not(mine))
            def _():
                left.wait_send() if wait else left.start()

            if not wait:
                @pl.when(mine)
                def _():
                    RL[row, core] = SB[b, h]

            mine_r = jnp.logical_and(b == cc, h == core)
            right = rc(SB.at[b, 2 + h], RR.at[cc, core], a_ss.at[k, 2 + h], a_rr.at[cc, core], (row, b * 2 + h))

            @pl.when(jnp.logical_not(mine_r))
            def _():
                right.wait_send() if wait else right.start()

            if not wait:
                @pl.when(mine_r)
                def _():
                    RR[cc, core] = SB[b, 2 + h]

    f_copy(0).wait()
    project(0)
    pl.semaphore_wait(bar, 29)
    scatter(0, False)

    def project_and_send(k, _):
        f_copy(k).wait()
        project(k)
        scatter(k, False)
        return 0

    lax.fori_loop(1, 8, project_and_send, 0)

    for g in range(8):
        WT[:, g * 128:(g + 1) * 128] = jnp.transpose(
            wout[g * 128:(g + 1) * 128, :].astype(F32)
        ).astype(BF16)
    bT[...] = jnp.transpose(
        jnp.concatenate([bias[...], jnp.zeros((126, 128), F32)], axis=0)
    )

    def clear(i, _):
        acc[i] = jnp.zeros((128, 256), F32)
        return 0

    lax.fori_loop(0, 32, clear, 0)

    for m in range(8):
        for k in range(2):
            @pl.when(jnp.logical_not(jnp.logical_and(m == cc, k == core)))
            def _():
                rc(RR.at[m, k], RR.at[m, k], a_ss.at[0, 0], a_rr.at[m, k], (row, col)).wait_recv()

    for ep in range(8):
        parts = [
            RR[m, k, 16 * ep:16 * ep + 16, :].astype(F32) for m in range(8) for k in range(2)
        ]
        for u in range(2):
            T[pl.ds(2 * ep + u, 128, stride=16), :] = jnp.transpose(
                jnp.concatenate([p[8 * u:8 * u + 8] for p in parts], axis=0)
            )
    e_half = pl.ds(pl.multiple_of(core * 16, 16), 16)
    SX[...] = T[pl.ds(pl.multiple_of((1 - core) * 1024, 1024), 1024), :].astype(BF16).reshape(64, 16, 128)
    sibling = dev(yh, x, yl, z, 1 - core)
    half_out = rc(SX, R.at[row, 2:66, e_half, :], x_ss, x_rs, sibling)
    half_out.start()
    R[row, 2:66, e_half, :] = T[pl.ds(pl.multiple_of(core * 1024, 1024), 1024), :].astype(BF16).reshape(64, 16, 128)
    mparts = jnp.concatenate(
        [RR[m, k, 128:144, :].astype(F32)[0:8] for m in range(8) for k in range(2)], axis=0
    )
    T[0:128, :] = jnp.transpose(mparts)
    R[row, 0:2] = T[pl.ds(pl.multiple_of(core * 64, 64), 64), :].astype(BF16).reshape(2, 32, 128)

    for n in range(8):
        for k in range(2):
            @pl.when(jnp.logical_not(jnp.logical_and(n == row, k == core)))
            def _():
                rc(RL.at[n, k], RL.at[n, k], a_ss.at[0, 0], a_rl.at[n, k], (row, col)).wait_recv()

    m_own = yl * 4 + z

    def rows_at(m):
        return pl.ds(pl.multiple_of(m * 16, 16), 16)

    def join(n, _):
        for g in range(8):
            a = RL[n, 0, 16 * g:16 * g + 16, :].astype(F32)
            b = RL[n, 1, 16 * g:16 * g + 16, :].astype(F32)
            for u in range(2):
                L[core, 2 * g + u, n, rows_at(m_own), :] = jnp.concatenate(
                    [a[8 * u:8 * u + 8], b[8 * u:8 * u + 8]], axis=0
                ).astype(BF16)
        return 0

    lax.fori_loop(0, 8, join, 0)
    for i in range(4):
        n = core * 4 + i
        a = RL[n, 0, 128:144, :].astype(F32)
        b = RL[n, 1, 128:144, :].astype(F32)
        Lm[n, rows_at(m_own), :] = jnp.concatenate([a[0:8], b[0:8]], axis=0).astype(BF16)

    sends = []

    def l_regions(q, h, m, half):
        lo, num = 2 * NG * q, 2 * NG
        n_lo, n_num = h * 4, 4
        if half is not None:
            num //= 2
            lo += half * num
            n_num //= 2
            n_lo = n_lo + half * n_num
        regions = [(q, L.at[h, lo:lo + num, :, rows_at(m), :])]
        if q == MQ:
            regions.append((Q, Lm.at[pl.ds(n_lo, n_num), rows_at(m), :]))
        return regions

    def l_send(q, m, half, to, slot):
        for i, ref in l_regions(q, core, m, half):
            c = rc(ref, ref, l_ss.at[i, slot], l_rs.at[i, slot], to)
            c.start()
            sends.append(c)

    def l_recv(q, h, m, half, slot):
        for i, ref in l_regions(q, h, m, half):
            rc(ref, ref, l_ss.at[i, slot], l_rs.at[i, slot], (row, col)).wait_recv()

    def r_region(p, n, half):
        lo = 0 if p == 0 else 2 + p * CJ
        num = CJ + 2 if p == 0 else CJ
        if half is not None:
            num //= 2
            lo += half * num
        return R.at[n, lo:lo + num]

    def r_send(p, n, half, to, slot):
        ref = r_region(p, n, half)
        c = rc(ref, ref, r_ss.at[p, slot], r_rs.at[p, slot], to)
        c.start()
        sends.append(c)

    def r_recv(p, n, half, slot):
        ref = r_region(p, n, half)
        rc(ref, ref, r_ss.at[p, slot], r_rs.at[p, slot], (row, col)).wait_recv()

    zu, zd, zo = lax.rem(z + 1, 4), lax.rem(z + 3, 4), lax.rem(z + 2, 4)
    xu, xd, xo = lax.rem(x + 1, 4), lax.rem(x + 3, 4), lax.rem(x + 2, 4)
    l_up, l_down = dev(yh, x, yl, zu, core), dev(yh, x, yl, zd, core)
    l_side = dev(yh, x, 1 - yl, z, core)
    r_up, r_down = dev(yh, xu, yl, z, core), dev(yh, xd, yl, z, core)
    r_side = dev(1 - yh, x, yl, z, core)
    ys = (yl, 1 - yl)
    hs = (yh, 1 - yh)

    def side(t):
        l_send(t, m_own, None, l_side, 0)
        r_send(t, row, None, r_side, 0)

    def first(t):
        l_send(t, m_own, None, l_up, 1)
        l_send(t, m_own, None, l_down, 2)
        r_send(t, row, None, r_up, 1)
        r_send(t, row, None, r_down, 2)
        l_send(t, m_own, None, sibling, 9)
        mp, np_ = ys[1] * 4 + z, hs[1] * 4 + x
        l_recv(t, core, mp, None, 0)
        l_send(t, mp, None, l_up, 3)
        l_send(t, mp, None, l_down, 4)
        r_recv(t, np_, None, 0)
        r_send(t, np_, None, r_up, 3)
        r_send(t, np_, None, r_down, 4)
        l_send(t, mp, None, sibling, 10)

    def second(t):
        for w in range(2):
            lu, ld = ys[w] * 4 + zu, ys[w] * 4 + zd
            ru, rd = hs[w] * 4 + xu, hs[w] * 4 + xd
            l_recv(t, core, ld, None, 1 + 2 * w)
            l_send(t, ld, 0, l_up, 5 + 2 * w)
            r_recv(t, rd, None, 1 + 2 * w)
            r_send(t, rd, 0, r_up, 5 + 2 * w)
            l_recv(t, core, lu, None, 2 + 2 * w)
            l_send(t, lu, 1, l_down, 6 + 2 * w)
            r_recv(t, ru, None, 2 + 2 * w)
            r_send(t, ru, 1, r_down, 6 + 2 * w)
            l_send(t, ld, None, sibling, 11 + 2 * w)
            l_send(t, lu, None, sibling, 12 + 2 * w)

    def third(t):
        for w in range(2):
            lo, ro = ys[w] * 4 + zo, hs[w] * 4 + xo
            l_recv(t, core, lo, 0, 5 + 2 * w)
            l_recv(t, core, lo, 1, 6 + 2 * w)
            l_send(t, lo, None, sibling, 15 + w)
            r_recv(t, ro, 0, 5 + 2 * w)
            r_recv(t, ro, 1, 6 + 2 * w)

    def fourth(t):
        for w in range(2):
            l_recv(t, 1 - core, ys[w] * 4 + z, None, 9 + w)
            l_recv(t, 1 - core, ys[w] * 4 + zd, None, 11 + 2 * w)
            l_recv(t, 1 - core, ys[w] * 4 + zu, None, 12 + 2 * w)
            l_recv(t, 1 - core, ys[w] * 4 + zo, None, 15 + w)

    def unit(q, p):
        lhs = jnp.concatenate(
            [R[n, pl.ds(2 + p * CJ, CJ)].reshape(CJ * 32, 128) for n in range(8)], axis=1
        )
        prods = []
        for gi in range(NG):
            for h in range(2):
                rhs = jnp.concatenate(
                    [L[h, (q * NG + gi) * 2 + u].reshape(1024, 128) for u in range(2)], axis=1
                )
                prods.append(jnp.dot(lhs, rhs, preferred_element_type=F32).astype(BF16))
        w = WT[:, pl.ds(pl.multiple_of(q * NG * 128, 128), NG * 128)]
        for jp in range(CJ // 2):
            blk = jnp.concatenate(
                [
                    jnp.concatenate(
                        [
                            o[j * 32:(j + 1) * 32, u * 128:(u + 1) * 128]
                            for o in prods for u in range(2)
                        ],
                        axis=0,
                    )
                    for j in (2 * jp, 2 * jp + 1)
                ],
                axis=1,
            )
            acc[p * (CJ // 2) + jp] += jnp.dot(w, blk, preferred_element_type=F32)

    def counts():
        total = jnp.zeros((64, 128), F32)
        for n in range(8):
            total = total + jnp.dot(
                R[n, 0:2].reshape(64, 128), Lm[n], preferred_element_type=F32
            )
        CT[...] = 1.0 / (total + 0.001)

    def out_copy(p):
        cols = pl.ds(pl.multiple_of(p * CJ, CJ), CJ)
        return pltpu.make_async_copy(out_v.at[:, cols, :], out.at[:, cols, :], o_sem.at[p])

    def finish(p):
        own = chain_rows[pl.ds(row, 1), :]
        for jp in range(CJ // 2):
            for u in range(2):
                j = 2 * jp + u
                a = acc[p * (CJ // 2) + jp, :, u * 128:(u + 1) * 128]
                a = a * CT[pl.ds(p * CJ + j, 1), :]
                same = own == chain_s[col * 64 + p * CJ + j]
                a = a + jnp.where(same, bT[:, 0:1], bT[:, 1:2])
                T[pl.ds(j, 128, stride=CJ), :] = jnp.transpose(a)
        cols = pl.ds(pl.multiple_of(p * CJ, CJ), CJ)
        out_v[:, cols, :] = (
            T[...].reshape(128, CJ, 128) + pair_v[:, cols, :].astype(F32)
        ).astype(BF16)
        out_copy(p).start()

    def compute(t):
        if t < Q - 1:
            if t > 0:
                lax.fori_loop(0, t, lambda q, _: (unit(q, t), 0)[1], 0)
            lax.fori_loop(0, t + 1, lambda p, _: (unit(t, p), 0)[1], 0)
        else:
            lax.fori_loop(0, t, lambda q, _: (unit(q, t), 0)[1], 0)
            counts()
            p_copy.wait()

            def last(p, _):
                unit(t, p)
                finish(p)
                return 0

            lax.fori_loop(0, Q, last, 0)

    rc(SX, R.at[row, 2:66, pl.ds(pl.multiple_of((1 - core) * 16, 16), 16), :], x_ss, x_rs, sibling).wait_recv()
    side(0)
    for t in range(Q + 2):
        if t + 1 < Q:
            side(t + 1)
        if t < Q:
            first(t)
        if 1 <= t <= Q:
            second(t - 1)
        if t >= 2:
            compute(t - 2)
        if 1 <= t <= Q:
            third(t - 1)
            fourth(t - 1)

    for c in sends:
        c.wait_send()
    half_out.wait_send()
    for k in range(8):
        scatter(k, True)
    for p in range(Q):
        out_copy(p).wait()


def per_device(
    homolog_features,
    presence_flags,
    residue_chain_index,
    pair_state,
    standardize_scale,
    standardize_shift,
    left_factor_matrix,
    right_factor_matrix,
    output_weight,
    chain_pair_bias,
):
    anywhere = pl.BlockSpec(memory_space=pl.ANY)
    vmem = pl.BlockSpec(memory_space=pltpu.VMEM)
    smem = pl.BlockSpec(memory_space=pltpu.SMEM)
    dma = pltpu.SemaphoreType.DMA
    return pl.pallas_call(
        kernel,
        out_shape=jax.ShapeDtypeStruct(pair_state.shape, BF16),
        in_specs=[anywhere, vmem, vmem, smem, anywhere, vmem, vmem, vmem, vmem, vmem, vmem],
        out_specs=anywhere,
        scratch_shapes=[
            pltpu.VMEM((8, 8, 128, 256), BF16),
            pltpu.VMEM((512, 128), F32),
            pltpu.VMEM((8, 4, 144, 128), BF16),
            pltpu.VMEM((8, 2, 144, 128), BF16),
            pltpu.VMEM((8, 2, 144, 128), BF16),
            pltpu.VMEM((2, 16, 8, 128, 128), BF16),
            pltpu.VMEM((8, 128, 128), BF16),
            pltpu.VMEM((8, 66, 32, 128), BF16),
            pltpu.VMEM((64, 16, 128), BF16),
            pltpu.VMEM((2048, 128), F32),
            pltpu.VMEM((128, 1024), BF16),
            pltpu.VMEM((64, 256), BF16),
            pltpu.VMEM((32, 128, 256), F32),
            pltpu.VMEM((64, 128), F32),
            pltpu.VMEM((128, 64, 128), BF16),
            pltpu.VMEM((128, 64, 128), BF16),
            pltpu.VMEM((128, 128), F32),
            dma((8,)), dma(()), dma((Q,)),
            dma((8, 4)), dma((8, 2)), dma((8, 2)), dma(()), dma(()),
            dma((Q + 1, 17)), dma((Q + 1, 17)), dma((Q, 9)), dma((Q, 9)),
        ],
        compiler_params=pltpu.CompilerParams(
            collective_id=0, has_side_effects=True, vmem_limit_bytes=60 << 20
        ),
    )(
        homolog_features, presence_flags, residue_chain_index.reshape(8, 128),
        residue_chain_index, pair_state, standardize_scale.reshape(1, -1),
        standardize_shift.reshape(1, -1), left_factor_matrix, right_factor_matrix,
        output_weight, chain_pair_bias,
    )


def solution(mesh):
    return jax.shard_map(
        per_device,
        mesh=mesh,
        in_specs=(
            P(("row", "col"), None, None),
            P(("row", "col"), None),
            P(),
            P("row", "col", None),
            P(),
            P(),
            P(),
            P(),
            P(),
            P(),
        ),
        out_specs=P("row", "col", None),
        check_vma=False,
    )
```

time: 369 us -> 105 us (0.28)
  Pallas kernels: 0 us -> 98.7 us
  local copies, waits for them, and re-layouts: 101 us -> 5.97 us
  matrix products: 89.1 us -> 0 us
  blocking collectives: 83.5 us -> 0 us
  waiting for transfers between devices: 58.1 us -> 0 us
  other arithmetic: 17.8 us -> 0 us
  between operations: 13.7 us -> 0.01 us
  starting transfers between devices: 3.96 us -> 0 us
    pallas_call x0 -> x1, Pallas kernels: none -> 98.7 us  [per_device(): pl.pallas_call(kernel, out_shape=jax.ShapeDtypeStruct(pair_state.shape, B...]
    dot_general x25 -> x0, matrix products: 89.1 us -> none  [the longest x8 47.5 us: one_block(): jnp.einsum('icje,cez->ijz', outer_prod, out_matrix, preferred_element_typ...]
    reshape x10 -> x0, local copies, waits for them, and re-layouts: 66 us -> none  [the longest x8 64.9 us: one_block(): outer_prod.astype(jnp.bfloat16)]
    all_gather x2 -> x0, blocking collectives: 52.6 us -> none  [the longest x1 28.1 us: per_device(): cols_mask = lax.all_gather(right_mpart, 'row', axis=0, tiled=True)]
    all_gather x2 -> x0, waiting for transfers between devices: 49.6 us -> none  [the longest x1 49.6 us: per_device(): lax.all_gather(left_part, 'col', axis=0, tiled=True)]
    all_to_all x1 -> x0, blocking collectives: 30.9 us -> none  [per_device(): lax.all_to_all(send_values, ('row', 'col'), split_axis=0, concat_axis=0,...]
    dynamic_slice x10 -> x0, local copies, waits for them, and re-layouts: 12 us -> none  [the longest x8 10.5 us: pair_terms(): lax.map(one_block, (rows_left.reshape(row_count // sub_rows, sub_rows, ou...]
    slice x7 -> x0, local copies, waits for them, and re-layouts: 9.18 us -> none  [the longest x2 5.51 us: per_device(): right_part = got_values[:, outer_width:]]
  transfers between devices with their start and end apart: 3 -> 0, of which waited for: 2 -> 0; matrix products, arithmetic and copies ran while one was open for 2% -> 0% of each run, Pallas kernels for 0% -> 0%
where the time goes in v1:
time: 105 us
  Pallas kernels  98.7 us (94%)
  local copies, waits for them, and re-layouts  5.97 us (6%)
    pallas_call x1, Pallas kernels, per_device(): pl.pallas_call(kernel, out_shape=jax.ShapeDtypeStruct(pair_state.shape, B...  98.7 us
    unnamed x3, local copies, waits for them, and re-layouts  5.97 us

profile of v1, /device:TPU:1, one launch (start us, length us, event | category | flops | bytes accessed | tf_op | source)
XLA Modules:
  0.0 104.7 jit_solution(7666577168884090296)
XLA Ops:
  0.0 1.4 %copy.11.wl = bf16[256,32]{1,0:T(8,128)(2,1)} copy(bf16[256,32]{0,1:T(8,128)(2,1)} %param.16) | data formatting | bytes 32768 | tf_op args[6]
  1.5 1.4 %copy.12.wr = bf16[256,32]{1,0:T(8,128)(2,1)} copy(bf16[256,32]{0,1:T(8,128)(2,1)} %param.17) | data formatting | bytes 32768 | tf_op args[7]
  2.9 98.7 %shard_map.100 = bf16[128,64,128]{2,1,0:T(8,128)(2,1)} custom-call(bf16[8,1024,256]{2,1,0:T(8,128)(2,1)} %feats.1, s32[8,1024]{1,0:T(8,128)} %flags.1, s32[8,128]{1,0:T(8,128)} %bitcast.3, s32[1024]{0:T(1024)} %chain_s.1, bf16[128,64,128]{2,1,0:T(8,128)(2,1)} %pair.1, f32[1,256]{1,0:T(1,128)} %bitcast.4, f32[1,256]{1,0:T(1,128)} %bitcast.5, ...), custom_call_target="tpu_custom_call" | custom-call | tf_op jit(solution)/shard_map/pallas_call | solution.py:413
  101.6 3.1 %copy.14 = bf16[128,64,128]{2,1,0:T(8,128)(2,1)} copy(bf16[128,64,128]{2,1,0:T(8,128)(2,1)} %shard_map.100) | data formatting | bytes 4194304

commit v2 on v1

--- a/solution.py
+++ b/solution.py
@@ -60,9 +60,8 @@
     p_copy = pltpu.make_async_copy(pair, pair_v, p_sem)
     p_copy.start()
 
-    PT[...] = jnp.transpose(
-        jnp.concatenate([wl[...].astype(F32), wr[...].astype(F32)], axis=1)
-    ).astype(BF16)
+    PT[0:32, :] = wl[...]
+    PT[32:64, :] = wr[...]
 
     def project(k):
         b = block_of(k)
@@ -114,18 +113,14 @@
                 def _():
                     RR[cc, core] = SB[b, 2 + h]
 
-    f_copy(0).wait()
-    project(0)
-    pl.semaphore_wait(bar, 29)
-    scatter(0, False)
-
-    def project_and_send(k, _):
+    def project_block(k, _):
         f_copy(k).wait()
         project(k)
-        scatter(k, False)
         return 0
 
-    lax.fori_loop(1, 8, project_and_send, 0)
+    lax.fori_loop(0, 8, project_block, 0)
+    pl.semaphore_wait(bar, 29)
+    lax.fori_loop(0, 8, lambda k, _: (scatter(k, False), 0)[1], 0)
 
     for g in range(8):
         WT[:, g * 128:(g + 1) * 128] = jnp.transpose(
@@ -257,6 +252,8 @@
         r_send(t, row, None, r_up, 1)
         r_send(t, row, None, r_down, 2)
         l_send(t, m_own, None, sibling, 9)
+
+    def partner(t):
         mp, np_ = ys[1] * 4 + z, hs[1] * 4 + x
         l_recv(t, core, mp, None, 0)
         l_send(t, mp, None, l_up, 3)
@@ -372,18 +369,21 @@
 
     rc(SX, R.at[row, 2:66, pl.ds(pl.multiple_of((1 - core) * 16, 16), 16), :], x_ss, x_rs, sibling).wait_recv()
     side(0)
+    first(0)
+    side(1)
     for t in range(Q + 2):
+        if t + 2 < Q:
+            side(t + 2)
         if t + 1 < Q:
-            side(t + 1)
+            first(t + 1)
         if t < Q:
-            first(t)
+            partner(t)
         if 1 <= t <= Q:
             second(t - 1)
         if t >= 2:
+            third(t - 2)
+            fourth(t - 2)
             compute(t - 2)
-        if 1 <= t <= Q:
-            third(t - 1)
-            fourth(t - 1)
 
     for c in sends:
         c.wait_send()
@@ -443,7 +443,7 @@
     )(
         homolog_features, presence_flags, residue_chain_index.reshape(8, 128),
         residue_chain_index, pair_state, standardize_scale.reshape(1, -1),
-        standardize_shift.reshape(1, -1), left_factor_matrix, right_factor_matrix,
+        standardize_shift.reshape(1, -1), left_factor_matrix.T, right_factor_matrix.T,
         output_weight, chain_pair_bias,
     )
 

time: 105 us -> 93.8 us (0.89)
  Pallas kernels: 98.7 us -> 89.5 us
  local copies, waits for them, and re-layouts: 5.97 us -> 3.08 us
    pallas_call x1, Pallas kernels: 98.7 us -> 89.5 us  [per_device(): pl.pallas_call(kernel, out_shape=jax.ShapeDtypeStruct(pair_state.shape, B...]
    unnamed x3 -> x1, local copies, waits for them, and re-layouts: 5.97 us -> 3.08 us
where the time goes in v2:
time: 93.8 us; the launch traced here: 92.6 us
  Pallas kernels  89.5 us (95%)
  local copies, waits for them, and re-layouts  3.08 us (3%)
    pallas_call x1, Pallas kernels, per_device(): pl.pallas_call(kernel, out_shape=jax.ShapeDtypeStruct(pair_state.shape, B...  89.5 us
    unnamed x1, local copies, waits for them, and re-layouts  3.08 us

profile of v2, /device:TPU:1, one launch (start us, length us, event | category | flops | bytes accessed | tf_op | source)
XLA Modules:
  0.0 92.6 jit_solution(64365563217249849)
XLA Ops:
  0.0 89.5 %shard_map.100 = bf16[128,64,128]{2,1,0:T(8,128)(2,1)} custom-call(bf16[8,1024,256]{2,1,0:T(8,128)(2,1)} %feats.1, s32[8,1024]{1,0:T(8,128)} %flags.1, s32[8,128]{1,0:T(8,128)} %bitcast.7, s32[1024]{0:T(1024)} %chain_s.1, bf16[128,64,128]{2,1,0:T(8,128)(2,1)} %pair.1, f32[1,256]{1,0:T(1,128)} %bitcast.8, f32[1,256]{1,0:T(1,128)} %bitcast.9, ...), custom_call_target="tpu_custom_call" | custom-call | tf_op jit(solution)/shard_map/pallas_call | solution.py:413
  89.5 3.1 %copy.12 = bf16[128,64,128]{2,1,0:T(8,128)(2,1)} copy(bf16[128,64,128]{2,1,0:T(8,128)(2,1)} %shard_map.100) | data formatting | bytes 4194304

commit v3 on v2

v3 whole, which is shorter than its diff:
```python
import jax
import jax.numpy as jnp
from jax import lax
from jax.experimental import pallas as pl
from jax.experimental.pallas import tpu as pltpu
from jax.sharding import PartitionSpec as P

MESH = pl.DeviceIdType.MESH
F32 = jnp.float32
BF16 = jnp.bfloat16
LEFT = ((0, 2), (2, 2), (4, 1), (5, 1), (6, 1), (7, 1))
RIGHT = ((0, 16), (16, 16), (32, 8), (40, 8), (48, 8), (56, 8))
ORDER = (
    "start", "al1out", "prep", "join0", "lS0", "lO0", "turn", "lG0", "halfw", "rS0", "rO0",
    "rO1", "join1", "lO1", "lP0", "lS1", "rG0", "lG1", "rP0", "rS1", "rG1", "lH0", "lO2", "lP1",
    "lS2", "lL0", "rP1", "rH0", "rS2", "rO2", "lG2", "lP2", "lS3", "lZ0", "rP2", "rS3", "lH1",
    "lO3", "rH1", "rO3", "lP3", "lS4", "rP3", "rZ0", "rS4", "u0.2.0.16", "rG2", "lH2", "lO4",
    "lP4", "lS5", "lL1", "rH2", "rO4", "rP4", "rS5", "lG3", "rZ1", "u0.2.16.16", "lZ1", "lL2",
    "rG3", "lH3", "lO5", "lP5", "rP5", "u2.2.0.16", "lZ2", "rH3", "lG4", "rO5", "u2.2.16.16",
    "rZ2", "lH4", "lL3", "rG4", "lG5", "rH4", "lZ3", "u4.2.0.16", "lH5", "u4.2.16.16", "rZ3",
    "lL4", "rH5", "u0.2.32.16", "rG5", "lL5", "u2.2.32.16", "lZ4", "rZ4", "u4.2.32.16", "lZ5",
    "rZ5", "u0.2.48.16", "u2.2.48.16", "u4.2.48.16", "u6.2.0.16", "f0", "u6.2.16.16", "f1",
    "u6.2.32.16", "f2", "u6.2.48.16", "f3",
)
Q = len(LEFT)
MQ = 1
PART = 48
CJ = 16


def kernel(
    feats, flags_h, chain_h, pair, scale_h, shift_h, wl, wr, wout_h, bias_h,
    out,
    F, Y, SL, SR, RL, RR, L, Lm, R, SX, T, WT, PT, acc, CT, SM, pair_v, bT,
    flags, chain, scale, shift, wout, bias,
    f_sem, i_sem, a_ss, a_rl, a_rr, x_ss, x_rs, l_ss, l_rs, r_ss, r_rs,
):
    row = lax.axis_index("row")
    col = lax.axis_index("col")
    yh, x = row // 4, row % 4
    cc, core = col // 2, col % 2
    yl, z = cc // 4, cc % 4

    def dev(yh_, x_, yl_, z_, k_):
        return (yh_ * 4 + x_, yl_ * 8 + z_ * 2 + k_)

    def rc(src, dst, ss, rs, d):
        return pltpu.make_async_remote_copy(
            src_ref=src, dst_ref=dst, send_sem=ss, recv_sem=rs, device_id=d, device_id_type=MESH
        )

    bar = pltpu.get_barrier_semaphore()
    for d in range(1, 16):
        at = lax.rem(row * 2 + core + d, 16)
        pl.semaphore_signal(
            bar, inc=1, device_id=(at // 2, cc * 2 + at % 2), device_id_type=MESH
        )
    for d in range(1, 8):
        for k in range(2):
            pl.semaphore_signal(
                bar, inc=1, device_id=(row, lax.rem(cc + d, 8) * 2 + k), device_id_type=MESH
            )

    def block_of(k):
        return lax.rem(row + cc + k, 8)

    def f_copy(k):
        b = block_of(k)
        return pltpu.make_async_copy(
            feats.at[:, pl.ds(pl.multiple_of(b * 128, 128), 128), :], F.at[k], f_sem.at[k]
        )

    loads = [
        pltpu.make_async_copy(src, dst, i_sem.at[i])
        for i, (src, dst) in enumerate((
            (flags_h, flags), (scale_h, scale), (shift_h, shift),
            (wl, PT.at[0:32]), (wr, PT.at[32:64]),
            (wout_h, wout), (bias_h, bias), (chain_h, chain), (pair, pair_v),
        ))
    ]
    for c in loads[:5]:
        c.start()
    for k in range(8):
        f_copy(k).start()
    for c in loads[5:]:
        c.start()
    for c in loads[:5]:
        c.wait()

    def project(k, _):
        f_copy(k).wait()
        b = block_of(k)
        present = flags[:, pl.ds(pl.multiple_of(b * 128, 128), 128)].astype(F32)
        for sp in range(4):
            v = F[k, 2 * sp:2 * sp + 2].reshape(256, 256).astype(F32)
            mu = jnp.mean(v, axis=-1, keepdims=True)
            d = v - mu
            var = jnp.mean(d * d, axis=-1, keepdims=True)
            nrm = (d * lax.rsqrt(var + 1e-05) * scale[...] + shift[...]).astype(BF16)
            pr = lax.dot_general(
                PT[...], nrm, (((1,), (1,)), ((), ())), preferred_element_type=F32
            )
            for u in range(2):
                s = 2 * sp + u
                Y[pl.ds(s, 64, stride=8), :] = pr[:, u * 128:(u + 1) * 128] * present[s:s + 1, :]
        pad = jnp.concatenate([present, jnp.zeros_like(present)], axis=0).astype(BF16)
        for h in range(2):
            SL[b, h, 0:16, :] = pad
            for g in range(8):
                at = (4 * g + 2 * h) * 8
                SL[b, h, 16 * g + 16:16 * g + 32, :] = Y[at:at + 16, :].astype(BF16)
            SR[b, h, 0:128, :] = Y[256 + h * 128:256 + (h + 1) * 128, :].astype(BF16)
            SR[b, h, 128:144, :] = pad
        return 0

    lax.fori_loop(0, 8, project, 0)

    def left_part(part):
        return slice(0, PART) if part == 0 else slice(PART, 144)

    def left_out(k, h, part):
        b = block_of(k)
        c = rc(
            SL.at[b, h, left_part(part)], RL.at[row, core, left_part(part)],
            a_ss.at[part, k, h], a_rl.at[part, row, core], (b, cc * 2 + h),
        )
        return c, jnp.logical_and(b == row, h == core)

    def right_out(k, h):
        b = block_of(k)
        c = rc(
            SR.at[b, h], RR.at[cc, core], a_ss.at[2, k, h], a_rr.at[cc, core], (row, b * 2 + h)
        )
        return c, jnp.logical_and(b == cc, h == core)

    def every(make, wait):
        def one(k, _):
            for h in range(2):
                c, mine = make(k, h)

                @pl.when(jnp.logical_not(mine))
                def _():
                    c.wait_send() if wait else c.start()

            return 0

        lax.fori_loop(0, 8, one, 0)

    pl.semaphore_wait(bar, 29)

    def start():
        every(lambda k, h: left_out(k, h, 0), False)
        every(right_out, False)
        RL[row, core] = SL[row, core]
        RR[cc, core] = SR[cc, core]

    def prepare():
        for c in loads[5:8]:
            c.wait()
        for g in range(8):
            WT[:, g * 128:(g + 1) * 128] = jnp.transpose(
                wout[g * 128:(g + 1) * 128, :].astype(F32)
            ).astype(BF16)
        bT[...] = jnp.transpose(
            jnp.concatenate([bias[...], jnp.zeros((126, 128), F32)], axis=0)
        )
        T[0:128, :] = jnp.transpose(
            jnp.broadcast_to(chain[pl.ds(cc, 1), :].astype(F32), (128, 128))
        )
        SM[...] = jnp.where(
            T[pl.ds(pl.multiple_of(core * 64, 64), 64), :] == chain[pl.ds(row, 1), :].astype(F32),
            1.0, 0.0,
        )

        def clear(i, _):
            acc[i] = jnp.zeros((128, 256), F32)
            return 0

        lax.fori_loop(0, 32, clear, 0)

    m_own = yl * 4 + z

    def rows_at(m):
        return pl.ds(pl.multiple_of(m * 16, 16), 16)

    def left_in(part):
        for n in range(8):
            for k in range(2):
                @pl.when(jnp.logical_not(jnp.logical_and(n == row, k == core)))
                def _():
                    ref = RL.at[n, k, left_part(part)]
                    rc(ref, ref, a_ss.at[0, 0, 0], a_rl.at[part, n, k], (row, col)).wait_recv()

    def join(n, g):
        a = RL[n, 0, 16 * g + 16:16 * g + 32, :].astype(F32)
        b = RL[n, 1, 16 * g + 16:16 * g + 32, :].astype(F32)
        for u in range(2):
            L[core, 2 * g + u, n, rows_at(m_own), :] = jnp.concatenate(
                [a[8 * u:8 * u + 8], b[8 * u:8 * u + 8]], axis=0
            ).astype(BF16)

    def join_groups(gs):
        def one(n, _):
            for g in gs:
                join(n, g)
            return 0

        lax.fori_loop(0, 8, one, 0)

    e_half = pl.ds(pl.multiple_of(core * 16, 16), 16)
    e_other = pl.ds(pl.multiple_of((1 - core) * 16, 16), 16)
    sibling = dev(yh, x, yl, z, 1 - core)
    half_out = rc(SX, R.at[row, 2:66, e_half, :], x_ss, x_rs, sibling)

    def turn():
        for m in range(8):
            for k in range(2):
                @pl.when(jnp.logical_not(jnp.logical_and(m == cc, k == core)))
                def _():
                    ref = RR.at[m, k]
                    rc(ref, ref, a_ss.at[0, 0, 0], a_rr.at[m, k], (row, col)).wait_recv()
        for ep in range(8):
            parts = [
                RR[m, k, 16 * ep:16 * ep + 16, :].astype(F32) for m in range(8) for k in range(2)
            ]
            for u in range(2):
                T[pl.ds(2 * ep + u, 128, stride=16), :] = jnp.transpose(
                    jnp.concatenate([p[8 * u:8 * u + 8] for p in parts], axis=0)
                )
        SX[...] = (
            T[pl.ds(pl.multiple_of((1 - core) * 1024, 1024), 1024), :]
            .astype(BF16).reshape(64, 16, 128)
        )
        half_out.start()
        R[row, 2:66, e_half, :] = (
            T[pl.ds(pl.multiple_of(core * 1024, 1024), 1024), :].astype(BF16).reshape(64, 16, 128)
        )
        present = jnp.concatenate(
            [RR[m, k, 128:144, :].astype(F32)[0:8] for m in range(8) for k in range(2)], axis=0
        )
        T[0:128, :] = jnp.transpose(present)
        R[row, 0:2] = (
            T[pl.ds(pl.multiple_of(core * 64, 64), 64), :].astype(BF16).reshape(2, 32, 128)
        )

    sends = []

    def l_regions(q, h, m, half):
        lo, num = 2 * LEFT[q][0], 2 * LEFT[q][1]
        n_lo, n_num = h * 4, 4
        if half is not None:
            num //= 2
            lo += half * num
            n_num //= 2
            n_lo = n_lo + half * n_num
        regions = [(q, L.at[h, lo:lo + num, :, rows_at(m), :])]
        if q == MQ:
            regions.append((Q, Lm.at[pl.ds(n_lo, n_num), rows_at(m), :]))
        return regions

    def l_send(q, m, half, to, slot):
        for i, ref in l_regions(q, core, m, half):
            c = rc(ref, ref, l_ss.at[i, slot], l_rs.at[i, slot], to)
            c.start()
            sends.append(c)

    def l_recv(q, h, m, half, slot):
        for i, ref in l_regions(q, h, m, half):
            rc(ref, ref, l_ss.at[i, slot], l_rs.at[i, slot], (row, col)).wait_recv()

    def r_region(p, n, half):
        lo, num = RIGHT[p][0] + 2, RIGHT[p][1]
        if p == 0:
            lo, num = 0, num + 2
        if half is not None:
            num //= 2
            lo += half * num
        return R.at[n, lo:lo + num]

    def r_send(p, n, half, to, slot):
        ref = r_region(p, n, half)
        c = rc(ref, ref, r_ss.at[p, slot], r_rs.at[p, slot], to)
        c.start()
        sends.append(c)

    def r_recv(p, n, half, slot):
        ref = r_region(p, n, half)
        rc(ref, ref, r_ss.at[p, slot], r_rs.at[p, slot], (row, col)).wait_recv()

    zu, zd, zo = lax.rem(z + 1, 4), lax.rem(z + 3, 4), lax.rem(z + 2, 4)
    xu, xd, xo = lax.rem(x + 1, 4), lax.rem(x + 3, 4), lax.rem(x + 2, 4)
    l_up, l_down = dev(yh, x, yl, zu, core), dev(yh, x, yl, zd, core)
    l_side = dev(yh, x, 1 - yl, z, core)
    r_up, r_down = dev(yh, xu, yl, z, core), dev(yh, xd, yl, z, core)
    r_side = dev(1 - yh, x, yl, z, core)
    ys = (yl, 1 - yl)
    hs = (yh, 1 - yh)
    mp, np_ = ys[1] * 4 + z, hs[1] * 4 + x

    def l_side_out(t):
        l_send(t, m_own, None, l_side, 0)

    def r_side_out(t):
        r_send(t, row, None, r_side, 0)

    def l_own(t):
        l_send(t, m_own, None, l_up, 1)
        l_send(t, m_own, None, l_down, 2)
        l_send(t, m_own, None, sibling, 9)

    def r_own(t):
        r_send(t, row, None, r_up, 1)
        r_send(t, row, None, r_down, 2)

    def l_partner(t):
        l_recv(t, core, mp, None, 0)
        l_send(t, mp, None, l_up, 3)
        l_send(t, mp, None, l_down, 4)
        l_send(t, mp, None, sibling, 10)

    def r_partner(t):
        r_recv(t, np_, None, 0)
        r_send(t, np_, None, r_up, 3)
        r_send(t, np_, None, r_down, 4)

    def l_far(t, w):
        lu, ld = ys[w] * 4 + zu, ys[w] * 4 + zd
        l_recv(t, core, ld, None, 1 + 2 * w)
        l_send(t, ld, 0, l_up, 5 + 2 * w)
        l_recv(t, core, lu, None, 2 + 2 * w)
        l_send(t, lu, 1, l_down, 6 + 2 * w)
        l_send(t, ld, None, sibling, 11 + 2 * w)
        l_send(t, lu, None, sibling, 12 + 2 * w)

    def r_far(t, w):
        ru, rd = hs[w] * 4 + xu, hs[w] * 4 + xd
        r_recv(t, rd, None, 1 + 2 * w)
        r_send(t, rd, 0, r_up, 5 + 2 * w)
        r_recv(t, ru, None, 2 + 2 * w)
        r_send(t, ru, 1, r_down, 6 + 2 * w)

    def l_last(t):
        for w in range(2):
            lo = ys[w] * 4 + zo
            l_recv(t, core, lo, 0, 5 + 2 * w)
            l_recv(t, core, lo, 1, 6 + 2 * w)
            l_send(t, lo, None, sibling, 15 + w)

    def r_done(t):
        for w in range(2):
            ro = hs[w] * 4 + xo
            r_recv(t, ro, 0, 5 + 2 * w)
            r_recv(t, ro, 1, 6 + 2 * w)

    def l_done(t):
        for w in range(2):
            l_recv(t, 1 - core, ys[w] * 4 + z, None, 9 + w)
            l_recv(t, 1 - core, ys[w] * 4 + zd, None, 11 + 2 * w)
            l_recv(t, 1 - core, ys[w] * 4 + zu, None, 12 + 2 * w)
            l_recv(t, 1 - core, ys[w] * 4 + zo, None, 15 + w)

    def unit(g0, ng, j0, nj):
        lhs = jnp.concatenate(
            [R[n, pl.ds(2 + j0, nj)].reshape(nj * 32, 128) for n in range(8)], axis=1
        )
        for s0 in range(0, ng, 2):
            sn = min(2, ng - s0)
            prods = []
            for gi in range(sn):
                for h in range(2):
                    rhs = jnp.concatenate(
                        [L[h, (g0 + s0 + gi) * 2 + u].reshape(1024, 128) for u in range(2)], axis=1
                    )
                    prods.append(jnp.dot(lhs, rhs, preferred_element_type=F32).astype(BF16))
            w = WT[:, (g0 + s0) * 128:(g0 + s0 + sn) * 128]
            for jp in range(nj // 2):
                blk = jnp.concatenate(
                    [
                        jnp.concatenate(
                            [
                                o[j * 32:(j + 1) * 32, u * 128:(u + 1) * 128]
                                for o in prods for u in range(2)
                            ],
                            axis=0,
                        )
                        for j in (2 * jp, 2 * jp + 1)
                    ],
                    axis=1,
                )
                acc[j0 // 2 + jp] += jnp.dot(w, blk, preferred_element_type=F32)

    def counts():
        total = jnp.zeros((64, 128), F32)
        for n in range(8):
            total = total + jnp.dot(
                R[n, 0:2].reshape(64, 128), Lm[n], preferred_element_type=F32
            )
        CT[...] = 1.0 / (total + 0.001)

    def finish(p):
        for jp in range(CJ // 2):
            for u in range(2):
                j = 2 * jp + u
                a = acc[p * (CJ // 2) + jp, :, u * 128:(u + 1) * 128]
                a = a * CT[p * CJ + j:p * CJ + j + 1, :]
                same = SM[p * CJ + j:p * CJ + j + 1, :] > 0.5
                a = a + jnp.where(same, bT[:, 0:1], bT[:, 1:2])
                T[pl.ds(j, 128, stride=CJ), :] = jnp.transpose(a)
        cols = slice(p * CJ, (p + 1) * CJ)
        out[:, cols, :] = (
            T[...].reshape(128, CJ, 128) + pair_v[:, cols, :].astype(F32)
        ).astype(BF16)

    def join_first():
        left_in(0)
        join_groups((0, 1))
        for i in range(4):
            n = core * 4 + i
            a = RL[n, 0, 0:16, :].astype(F32)
            b = RL[n, 1, 0:16, :].astype(F32)
            Lm[n, rows_at(m_own), :] = jnp.concatenate([a[0:8], b[0:8]], axis=0).astype(BF16)

    def join_rest():
        left_in(1)
        join_groups((2, 3, 4, 5, 6, 7))

    def half_in():
        rc(SX, R.at[row, 2:66, e_other, :], x_ss, x_rs, sibling).wait_recv()

    def finish_from(p):
        if not finished:
            counts()
            loads[8].wait()
        finished.append(p)
        finish(p)

    finished = []
    once = {
        "start": start, "prep": prepare, "join0": join_first, "join1": join_rest,
        "turn": turn, "halfw": half_in,
        "al1out": lambda: every(lambda k, h: left_out(k, h, 1), False),
    }
    steps = {
        "lS": l_side_out, "lO": l_own, "lP": l_partner, "lL": l_last, "lZ": l_done,
        "lG": lambda t: l_far(t, 0), "lH": lambda t: l_far(t, 1),
        "rS": r_side_out, "rO": r_own, "rP": r_partner, "rZ": r_done,
        "rG": lambda t: r_far(t, 0), "rH": lambda t: r_far(t, 1),
    }
    for name in ORDER:
        if name in once:
            once[name]()
        elif name[0] == "u":
            unit(*[int(v) for v in name[1:].split(".")])
        elif name[0] == "f":
            finish_from(int(name[1:]))
        else:
            steps[name[:2]](int(name[2:]))

    for c in sends:
        c.wait_send()
    half_out.wait_send()
    every(lambda k, h: left_out(k, h, 0), True)
    every(right_out, True)
    every(lambda k, h: left_out(k, h, 1), True)


def per_device(
    homolog_features,
    presence_flags,
    residue_chain_index,
    pair_state,
    standardize_scale,
    standardize_shift,
    left_factor_matrix,
    right_factor_matrix,
    output_weight,
    chain_pair_bias,
):
    anywhere = pl.BlockSpec(memory_space=pl.ANY)
    dma = pltpu.SemaphoreType.DMA
    return pl.pallas_call(
        kernel,
        out_shape=pltpu.VMEM(pair_state.shape, BF16),
        in_specs=[anywhere] * 10,
        out_specs=pl.BlockSpec(memory_space=pltpu.VMEM),
        scratch_shapes=[
            pltpu.VMEM((8, 8, 128, 256), BF16),
            pltpu.VMEM((512, 128), F32),
            pltpu.VMEM((8, 2, 144, 128), BF16),
            pltpu.VMEM((8, 2, 144, 128), BF16),
            pltpu.VMEM((8, 2, 144, 128), BF16),
            pltpu.VMEM((8, 2, 144, 128), BF16),
            pltpu.VMEM((2, 16, 8, 128, 128), BF16),
            pltpu.VMEM((8, 128, 128), BF16),
            pltpu.VMEM((8, 66, 32, 128), BF16),
            pltpu.VMEM((64, 16, 128), BF16),
            pltpu.VMEM((2048, 128), F32),
            pltpu.VMEM((128, 1024), BF16),
            pltpu.VMEM((64, 256), BF16),
            pltpu.VMEM((32, 128, 256), F32),
            pltpu.VMEM((64, 128), F32),
            pltpu.VMEM((64, 128), F32),
            pltpu.VMEM((128, 64, 128), BF16),
            pltpu.VMEM((128, 128), F32),
            pltpu.VMEM((8, 1024), jnp.int32),
            pltpu.VMEM((8, 128), jnp.int32),
            pltpu.VMEM((1, 256), F32),
            pltpu.VMEM((1, 256), F32),
            pltpu.VMEM((1024, 128), BF16),
            pltpu.VMEM((2, 128), F32),
            dma((8,)), dma((9,)),
            dma((3, 8, 2)), dma((2, 8, 2)), dma((8, 2)), dma(()), dma(()),
            dma((Q + 1, 17)), dma((Q + 1, 17)), dma((Q, 9)), dma((Q, 9)),
        ],
        compiler_params=pltpu.CompilerParams(
            collective_id=0, has_side_effects=True, vmem_limit_bytes=61 << 20
        ),
    )(
        homolog_features, presence_flags, residue_chain_index.reshape(8, 128),
        pair_state, standardize_scale.reshape(1, -1),
        standardize_shift.reshape(1, -1), left_factor_matrix.T, right_factor_matrix.T,
        output_weight, chain_pair_bias,
    )


def solution(mesh):
    return jax.shard_map(
        per_device,
        mesh=mesh,
        in_specs=(
            P(("row", "col"), None, None),
            P(("row", "col"), None),
            P(),
            P("row", "col", None),
            P(),
            P(),
            P(),
            P(),
            P(),
            P(),
        ),
        out_specs=P("row", "col", None),
        check_vma=False,
    )
```

time: 93.8 us -> 87.1 us (0.929); the launches traced: 92.6 us -> 87 us
  Pallas kernels: 89.5 us -> 85.6 us
  local copies, waits for them, and re-layouts: 3.08 us -> 1.32 us
    pallas_call x1, Pallas kernels: 89.5 us -> 85.6 us  [per_device(): pl.pallas_call(kernel, out_shape=pltpu.VMEM(pair_state.shape, BF16), in_s...]
    unnamed x1, local copies, waits for them, and re-layouts: 3.08 us -> 1.32 us
where the time goes in v3:
time: 87.1 us; the launch traced here: 87 us
  Pallas kernels  85.6 us (98%)
  local copies, waits for them, and re-layouts  1.32 us (2%)
    pallas_call x1, Pallas kernels, per_device(): pl.pallas_call(kernel, out_shape=pltpu.VMEM(pair_state.shape, BF16), in_s...  85.6 us

profile of v3, /device:TPU:1, one launch (start us, length us, event | category | flops | bytes accessed | tf_op | source)
XLA Modules:
  0.0 87.0 jit_solution(3785268786309598729)
XLA Ops:
  0.0 85.6 %shard_map.100 = bf16[128,64,128]{2,1,0:T(8,128)(2,1)S(1)} custom-call(bf16[8,1024,256]{2,1,0:T(8,128)(2,1)} %feats.1, s32[8,1024]{1,0:T(8,128)} %flags_h.1, s32[8,128]{1,0:T(8,128)} %bitcast.7, bf16[128,64,128]{2,1,0:T(8,128)(2,1)} %pair.1, f32[1,256]{1,0:T(1,128)} %bitcast.8, f32[1,256]{1,0:T(1,128)} %bitcast.9, bf16[32,256]{1,0:T(8,128)(2,1)} %bitcast.5, ...), custom_call_target="tpu_custom_call" | custom-call | tf_op jit(solution)/shard_map/pallas_call | solution.py:481
  85.6 1.3 %copy.12 = bf16[128,64,128]{2,1,0:T(8,128)(2,1)} copy(bf16[128,64,128]{2,1,0:T(8,128)(2,1)S(1)} %shard_map.100) | data formatting | bytes 4194304

commit v4 on v3

--- a/solution.py
+++ b/solution.py
@@ -3,26 +3,26 @@
 from jax import lax
 from jax.experimental import pallas as pl
 from jax.experimental.pallas import tpu as pltpu
-from jax.sharding import PartitionSpec as P
+from jax.sharding import PartitionSpec as Spec
 
 MESH = pl.DeviceIdType.MESH
 F32 = jnp.float32
 BF16 = jnp.bfloat16
-LEFT = ((0, 2), (2, 2), (4, 1), (5, 1), (6, 1), (7, 1))
-RIGHT = ((0, 16), (16, 16), (32, 8), (40, 8), (48, 8), (56, 8))
+LEFT = ((0, 2), (2, 2), (4, 2), (6, 1), (7, 1))
+RIGHT = ((0, 16), (16, 16), (32, 16), (48, 8), (56, 8))
 ORDER = (
-    "start", "al1out", "prep", "join0", "lS0", "lO0", "turn", "lG0", "halfw", "rS0", "rO0",
-    "rO1", "join1", "lO1", "lP0", "lS1", "rG0", "lG1", "rP0", "rS1", "rG1", "lH0", "lO2", "lP1",
-    "lS2", "lL0", "rP1", "rH0", "rS2", "rO2", "lG2", "lP2", "lS3", "lZ0", "rP2", "rS3", "lH1",
-    "lO3", "rH1", "rO3", "lP3", "lS4", "rP3", "rZ0", "rS4", "u0.2.0.16", "rG2", "lH2", "lO4",
-    "lP4", "lS5", "lL1", "rH2", "rO4", "rP4", "rS5", "lG3", "rZ1", "u0.2.16.16", "lZ1", "lL2",
-    "rG3", "lH3", "lO5", "lP5", "rP5", "u2.2.0.16", "lZ2", "rH3", "lG4", "rO5", "u2.2.16.16",
-    "rZ2", "lH4", "lL3", "rG4", "lG5", "rH4", "lZ3", "u4.2.0.16", "lH5", "u4.2.16.16", "rZ3",
-    "lL4", "rH5", "u0.2.32.16", "rG5", "lL5", "u2.2.32.16", "lZ4", "rZ4", "u4.2.32.16", "lZ5",
-    "rZ5", "u0.2.48.16", "u2.2.48.16", "u4.2.48.16", "u6.2.0.16", "f0", "u6.2.16.16", "f1",
-    "u6.2.32.16", "f2", "u6.2.48.16", "f3",
+    "start", "prep", "al1out", "join0", "lO0", "lS0", "turn", "rO0", "lR0", "lP0", "rS0", "rO1",
+    "join1", "lS1", "lO2", "lB0", "lH0", "lO1", "rG0", "rS1", "rP0", "lR1", "lG0", "lS2", "rG1",
+    "rS2", "lP1", "lO3", "rP1", "rO2", "lR2", "lL0", "lB1", "rH0", "lP2", "lZ0", "lH1", "rP2",
+    "rH1", "lG1", "lB2", "rG2", "rS3", "lH2", "lS4", "lS3", "rZ0", "u0.2.0.16", "rP3", "lL1",
+    "rS4", "rH2", "lR4", "rO4", "rO3", "lP4", "lR3", "lG2", "lP3", "lO4", "rZ1", "u0.2.16.16",
+    "lZ1", "u2.2.0.16", "rP4", "lB4", "u2.2.16.16", "lL2", "rH3", "lB3", "lH4", "rZ2",
+    "u0.2.32.16", "lH3", "u2.2.32.16", "rG4", "lG4", "rG3", "lZ2", "u4.2.16.16", "lG3", "rH4",
+    "u4.2.32.16", "u4.2.0.16", "lL4", "rZ3", "lL3", "rZ4", "u4.2.48.16", "u2.2.48.16", "lZ4",
+    "u0.2.48.16", "lZ3", "u6.2.16.16", "f1", "u6.2.0.16", "f0", "u6.2.48.16", "f3",
+    "u6.2.32.16", "f2",
 )
-Q = len(LEFT)
+Q, P = len(LEFT), len(RIGHT)
 MQ = 1
 PART = 48
 CJ = 16
@@ -31,9 +31,9 @@
 def kernel(
     feats, flags_h, chain_h, pair, scale_h, shift_h, wl, wr, wout_h, bias_h,
     out,
-    F, Y, SL, SR, RL, RR, L, Lm, R, SX, T, WT, PT, acc, CT, SM, pair_v, bT,
+    F, Y, SL, SR, RL, RR, L, Lm, LX, LXm, R, T, WT, PT, acc, CT, SM, pair_v, bT,
     flags, chain, scale, shift, wout, bias,
-    f_sem, i_sem, a_ss, a_rl, a_rr, x_ss, x_rs, l_ss, l_rs, r_ss, r_rs,
+    f_sem, i_sem, a_ss, a_rl, a_rr, l_ss, l_rs, r_ss, r_rs,
 ):
     row = lax.axis_index("row")
     col = lax.axis_index("col")
@@ -50,16 +50,13 @@
         )
 
     bar = pltpu.get_barrier_semaphore()
-    for d in range(1, 16):
-        at = lax.rem(row * 2 + core + d, 16)
-        pl.semaphore_signal(
-            bar, inc=1, device_id=(at // 2, cc * 2 + at % 2), device_id_type=MESH
-        )
-    for d in range(1, 8):
-        for k in range(2):
-            pl.semaphore_signal(
-                bar, inc=1, device_id=(row, lax.rem(cc + d, 8) * 2 + k), device_id_type=MESH
-            )
+    greeted = [(row, lax.rem(col + d, 16)) for d in range(1, 16)]
+    greeted += [
+        (yh * 4 + lax.rem(x + d, 4), cc * 2 + k) for d in range(1, 4) for k in range(2)
+    ]
+    greeted += [dev(1 - yh, x, yl, z, core), dev(1 - yh, x, 1 - yl, z, core)]
+    for d in greeted:
+        pl.semaphore_signal(bar, inc=1, device_id=d, device_id_type=MESH)
 
     def block_of(k):
         return lax.rem(row + cc + k, 8)
@@ -109,8 +106,17 @@
             for g in range(8):
                 at = (4 * g + 2 * h) * 8
                 SL[b, h, 16 * g + 16:16 * g + 32, :] = Y[at:at + 16, :].astype(BF16)
-            SR[b, h, 0:128, :] = Y[256 + h * 128:256 + (h + 1) * 128, :].astype(BF16)
-            SR[b, h, 128:144, :] = pad
+        low = lax.broadcasted_iota(jnp.int32, (16, 128), 1) < 64
+        for g in range(8):
+            y = Y[256 + 32 * g:288 + 32 * g, :]
+            e0 = jnp.concatenate([y[0:8], y[16:24]], axis=0)
+            e1 = jnp.concatenate([y[8:16], y[24:32]], axis=0)
+            at = slice(16 * g, 16 * g + 16)
+            SR[b, 0, at, :] = jnp.where(low, e0, pltpu.roll(e1, 64, 1)).astype(BF16)
+            SR[b, 1, at, :] = jnp.where(low, pltpu.roll(e0, 64, 1), e1).astype(BF16)
+        both = jnp.concatenate([present, jnp.zeros_like(present)], axis=0)
+        SR[b, 0, 128:144, :] = pad
+        SR[b, 1, 128:144, :] = pltpu.roll(both, 64, 1).astype(BF16)
         return 0
 
     lax.fori_loop(0, 8, project, 0)
@@ -121,10 +127,11 @@
     def left_out(k, h, part):
         b = block_of(k)
         c = rc(
-            SL.at[b, h, left_part(part)], RL.at[row, core, left_part(part)],
-            a_ss.at[part, k, h], a_rl.at[part, row, core], (b, cc * 2 + h),
-        )
-        return c, jnp.logical_and(b == row, h == core)
+            SL.at[b, h, left_part(part)], RL.at[b // 4, x, core, left_part(part)],
+            a_ss.at[part, k, h], a_rl.at[part, b // 4, x, core],
+            (yh * 4 + lax.rem(b, 4), cc * 2 + h),
+        )
+        return c, jnp.logical_and(lax.rem(b, 4) == x, h == core)
 
     def right_out(k, h):
         b = block_of(k)
@@ -146,12 +153,13 @@
 
         lax.fori_loop(0, 8, one, 0)
 
-    pl.semaphore_wait(bar, 29)
+    pl.semaphore_wait(bar, len(greeted))
 
     def start():
         every(lambda k, h: left_out(k, h, 0), False)
         every(right_out, False)
-        RL[row, core] = SL[row, core]
+        for i in range(2):
+            RL[i, x, core] = SL[i * 4 + x, core]
         RR[cc, core] = SR[cc, core]
 
     def prepare():
@@ -184,33 +192,34 @@
         return pl.ds(pl.multiple_of(m * 16, 16), 16)
 
     def left_in(part):
-        for n in range(8):
-            for k in range(2):
-                @pl.when(jnp.logical_not(jnp.logical_and(n == row, k == core)))
-                def _():
-                    ref = RL.at[n, k, left_part(part)]
-                    rc(ref, ref, a_ss.at[0, 0, 0], a_rl.at[part, n, k], (row, col)).wait_recv()
-
-    def join(n, g):
-        a = RL[n, 0, 16 * g + 16:16 * g + 32, :].astype(F32)
-        b = RL[n, 1, 16 * g + 16:16 * g + 32, :].astype(F32)
-        for u in range(2):
-            L[core, 2 * g + u, n, rows_at(m_own), :] = jnp.concatenate(
-                [a[8 * u:8 * u + 8], b[8 * u:8 * u + 8]], axis=0
-            ).astype(BF16)
+        for i in range(2):
+            for n in range(4):
+                for k in range(2):
+                    @pl.when(jnp.logical_not(jnp.logical_and(n == x, k == core)))
+                    def _():
+                        ref = RL.at[i, n, k, left_part(part)]
+                        rc(ref, ref, a_ss.at[0, 0, 0], a_rl.at[part, i, n, k], (row, col)).wait_recv()
+
+    def joined(i, n, at):
+        a = RL[i, n, 0, at:at + 16, :].astype(F32)
+        b = RL[i, n, 1, at:at + 16, :].astype(F32)
+        return [
+            jnp.concatenate([a[8 * u:8 * u + 8], b[8 * u:8 * u + 8]], axis=0).astype(BF16)
+            for u in range(2)
+        ]
 
     def join_groups(gs):
         def one(n, _):
             for g in gs:
-                join(n, g)
+                for u, v in enumerate(joined(yh, n, 16 * g + 16)):
+                    L[core, 2 * g + u, yh * 4 + n, rows_at(m_own), :] = v
+                for u, v in enumerate(joined(1 - yh, n, 16 * g + 16)):
+                    LX[2 * g + u, n] = v
             return 0
 
-        lax.fori_loop(0, 8, one, 0)
-
-    e_half = pl.ds(pl.multiple_of(core * 16, 16), 16)
-    e_other = pl.ds(pl.multiple_of((1 - core) * 16, 16), 16)
+        lax.fori_loop(0, 4, one, 0)
+
     sibling = dev(yh, x, yl, z, 1 - core)
-    half_out = rc(SX, R.at[row, 2:66, e_half, :], x_ss, x_rs, sibling)
 
     def turn():
         for m in range(8):
@@ -219,53 +228,46 @@
                 def _():
                     ref = RR.at[m, k]
                     rc(ref, ref, a_ss.at[0, 0, 0], a_rr.at[m, k], (row, col)).wait_recv()
-        for ep in range(8):
+        for g in range(8):
             parts = [
-                RR[m, k, 16 * ep:16 * ep + 16, :].astype(F32) for m in range(8) for k in range(2)
+                RR[m, k, 16 * g:16 * g + 16, :].astype(F32) for m in range(8) for k in range(2)
             ]
             for u in range(2):
-                T[pl.ds(2 * ep + u, 128, stride=16), :] = jnp.transpose(
+                t = jnp.transpose(
                     jnp.concatenate([p[8 * u:8 * u + 8] for p in parts], axis=0)
                 )
-        SX[...] = (
-            T[pl.ds(pl.multiple_of((1 - core) * 1024, 1024), 1024), :]
-            .astype(BF16).reshape(64, 16, 128)
-        )
-        half_out.start()
-        R[row, 2:66, e_half, :] = (
-            T[pl.ds(pl.multiple_of(core * 1024, 1024), 1024), :].astype(BF16).reshape(64, 16, 128)
-        )
-        present = jnp.concatenate(
+                for i in range(2):
+                    T[pl.ds(4 * g + 2 * u + i, 64, stride=32), :] = t[64 * i:64 * i + 64]
+        R[row, 2:66] = T[...].astype(BF16).reshape(64, 32, 128)
+        t = jnp.transpose(jnp.concatenate(
             [RR[m, k, 128:144, :].astype(F32)[0:8] for m in range(8) for k in range(2)], axis=0
-        )
-        T[0:128, :] = jnp.transpose(present)
-        R[row, 0:2] = (
-            T[pl.ds(pl.multiple_of(core * 64, 64), 64), :].astype(BF16).reshape(2, 32, 128)
-        )
+        ))
+        R[row, 0:2] = t[0:64].astype(BF16).reshape(2, 32, 128)
 
     sends = []
 
-    def l_regions(q, h, m, half):
+    ALL = slice(None)
+
+    def l_regions(q, h, m, part=None, yhalf=None):
         lo, num = 2 * LEFT[q][0], 2 * LEFT[q][1]
-        n_lo, n_num = h * 4, 4
-        if half is not None:
+        if part is not None:
             num //= 2
-            lo += half * num
-            n_num //= 2
-            n_lo = n_lo + half * n_num
-        regions = [(q, L.at[h, lo:lo + num, :, rows_at(m), :])]
+            lo += part * num
+        n = ALL if yhalf is None else pl.ds(yhalf * 4, 4)
+        regions = [(q, L.at[h, lo:lo + num, n, rows_at(m), :])]
         if q == MQ:
-            regions.append((Q, Lm.at[pl.ds(n_lo, n_num), rows_at(m), :]))
+            i = part if part is not None else ALL if yhalf is None else yhalf
+            regions.append((Q, Lm.at[i, pl.ds(h * 2, 2), rows_at(m), :]))
         return regions
 
-    def l_send(q, m, half, to, slot):
-        for i, ref in l_regions(q, core, m, half):
+    def l_send(q, m, to, slot, **which):
+        for i, ref in l_regions(q, core, m, **which):
             c = rc(ref, ref, l_ss.at[i, slot], l_rs.at[i, slot], to)
             c.start()
             sends.append(c)
 
-    def l_recv(q, h, m, half, slot):
-        for i, ref in l_regions(q, h, m, half):
+    def l_recv(q, h, m, slot, **which):
+        for i, ref in l_regions(q, h, m, **which):
             rc(ref, ref, l_ss.at[i, slot], l_rs.at[i, slot], (row, col)).wait_recv()
 
     def r_region(p, n, half):
@@ -291,6 +293,7 @@
     xu, xd, xo = lax.rem(x + 1, 4), lax.rem(x + 3, 4), lax.rem(x + 2, 4)
     l_up, l_down = dev(yh, x, yl, zu, core), dev(yh, x, yl, zd, core)
     l_side = dev(yh, x, 1 - yl, z, core)
+    l_cross = dev(1 - yh, x, 1 - yl, z, core)
     r_up, r_down = dev(yh, xu, yl, z, core), dev(yh, xd, yl, z, core)
     r_side = dev(1 - yh, x, yl, z, core)
     ys = (yl, 1 - yl)
@@ -298,39 +301,62 @@
     mp, np_ = ys[1] * 4 + z, hs[1] * 4 + x
 
     def l_side_out(t):
-        l_send(t, m_own, None, l_side, 0)
+        l_send(t, m_own, l_side, 0, yhalf=yh)
+        lo, num = 2 * LEFT[t][0], 2 * LEFT[t][1]
+        away = [LX.at[lo:lo + num], LXm.at[pl.ds(core * 2, 2)]]
+        for src, (i, dst) in zip(away, l_regions(t, core, m_own, yhalf=yh)):
+            c = rc(src, dst, l_ss.at[i, 17], l_rs.at[i, 17], l_cross)
+            c.start()
+            sends.append(c)
+
+    def l_pass(t):
+        l_recv(t, core, mp, 17, yhalf=1 - yh)
+        l_send(t, mp, l_side, 18, yhalf=1 - yh)
 
     def r_side_out(t):
         r_send(t, row, None, r_side, 0)
 
     def l_own(t):
-        l_send(t, m_own, None, l_up, 1)
-        l_send(t, m_own, None, l_down, 2)
-        l_send(t, m_own, None, sibling, 9)
+        l_send(t, m_own, l_up, 1, yhalf=yh)
+        l_send(t, m_own, l_down, 2, yhalf=yh)
+        l_send(t, m_own, sibling, 9, yhalf=yh)
+
+    def l_own_rest(t):
+        l_recv(t, core, m_own, 18, yhalf=1 - yh)
+        l_send(t, m_own, l_up, 19, yhalf=1 - yh)
+        l_send(t, m_own, l_down, 20, yhalf=1 - yh)
+        l_send(t, m_own, sibling, 21, yhalf=1 - yh)
 
     def r_own(t):
         r_send(t, row, None, r_up, 1)
         r_send(t, row, None, r_down, 2)
 
     def l_partner(t):
-        l_recv(t, core, mp, None, 0)
-        l_send(t, mp, None, l_up, 3)
-        l_send(t, mp, None, l_down, 4)
-        l_send(t, mp, None, sibling, 10)
+        l_recv(t, core, mp, 0, yhalf=yh)
+        l_send(t, mp, l_up, 3)
+        l_send(t, mp, l_down, 4)
+        l_send(t, mp, sibling, 10)
 
     def r_partner(t):
         r_recv(t, np_, None, 0)
         r_send(t, np_, None, r_up, 3)
         r_send(t, np_, None, r_down, 4)
 
+    def l_near(t, m, slot, rest, w):
+        if w:
+            l_recv(t, core, m, slot + 2)
+        else:
+            l_recv(t, core, m, slot, yhalf=yh)
+            l_recv(t, core, m, rest, yhalf=1 - yh)
+
     def l_far(t, w):
         lu, ld = ys[w] * 4 + zu, ys[w] * 4 + zd
-        l_recv(t, core, ld, None, 1 + 2 * w)
-        l_send(t, ld, 0, l_up, 5 + 2 * w)
-        l_recv(t, core, lu, None, 2 + 2 * w)
-        l_send(t, lu, 1, l_down, 6 + 2 * w)
-        l_send(t, ld, None, sibling, 11 + 2 * w)
-        l_send(t, lu, None, sibling, 12 + 2 * w)
+        l_near(t, ld, 1, 19, w)
+        l_send(t, ld, l_up, 5 + 2 * w, part=0)
+        l_near(t, lu, 2, 20, w)
+        l_send(t, lu, l_down, 6 + 2 * w, part=1)
+        l_send(t, ld, sibling, 11 + 2 * w)
+        l_send(t, lu, sibling, 12 + 2 * w)
 
     def r_far(t, w):
         ru, rd = hs[w] * 4 + xu, hs[w] * 4 + xd
@@ -342,9 +368,9 @@
     def l_last(t):
         for w in range(2):
             lo = ys[w] * 4 + zo
-            l_recv(t, core, lo, 0, 5 + 2 * w)
-            l_recv(t, core, lo, 1, 6 + 2 * w)
-            l_send(t, lo, None, sibling, 15 + w)
+            l_recv(t, core, lo, 5 + 2 * w, part=0)
+            l_recv(t, core, lo, 6 + 2 * w, part=1)
+            l_send(t, lo, sibling, 15 + w)
 
     def r_done(t):
         for w in range(2):
@@ -353,11 +379,13 @@
             r_recv(t, ro, 1, 6 + 2 * w)
 
     def l_done(t):
+        l_recv(t, 1 - core, m_own, 9, yhalf=yh)
+        l_recv(t, 1 - core, m_own, 21, yhalf=1 - yh)
+        l_recv(t, 1 - core, mp, 10)
         for w in range(2):
-            l_recv(t, 1 - core, ys[w] * 4 + z, None, 9 + w)
-            l_recv(t, 1 - core, ys[w] * 4 + zd, None, 11 + 2 * w)
-            l_recv(t, 1 - core, ys[w] * 4 + zu, None, 12 + 2 * w)
-            l_recv(t, 1 - core, ys[w] * 4 + zo, None, 15 + w)
+            l_recv(t, 1 - core, ys[w] * 4 + zd, 11 + 2 * w)
+            l_recv(t, 1 - core, ys[w] * 4 + zu, 12 + 2 * w)
+            l_recv(t, 1 - core, ys[w] * 4 + zo, 15 + w)
 
     def unit(g0, ng, j0, nj):
         lhs = jnp.concatenate(
@@ -393,7 +421,7 @@
         total = jnp.zeros((64, 128), F32)
         for n in range(8):
             total = total + jnp.dot(
-                R[n, 0:2].reshape(64, 128), Lm[n], preferred_element_type=F32
+                R[n, 0:2].reshape(64, 128), Lm[n // 4, n % 4], preferred_element_type=F32
             )
         CT[...] = 1.0 / (total + 0.001)
 
@@ -414,18 +442,14 @@
     def join_first():
         left_in(0)
         join_groups((0, 1))
-        for i in range(4):
-            n = core * 4 + i
-            a = RL[n, 0, 0:16, :].astype(F32)
-            b = RL[n, 1, 0:16, :].astype(F32)
-            Lm[n, rows_at(m_own), :] = jnp.concatenate([a[0:8], b[0:8]], axis=0).astype(BF16)
+        for i in range(2):
+            n = core * 2 + i
+            Lm[yh, n, rows_at(m_own), :] = joined(yh, n, 0)[0]
+            LXm[n] = joined(1 - yh, n, 0)[0]
 
     def join_rest():
         left_in(1)
         join_groups((2, 3, 4, 5, 6, 7))
-
-    def half_in():
-        rc(SX, R.at[row, 2:66, e_other, :], x_ss, x_rs, sibling).wait_recv()
 
     def finish_from(p):
         if not finished:
@@ -437,11 +461,12 @@
     finished = []
     once = {
         "start": start, "prep": prepare, "join0": join_first, "join1": join_rest,
-        "turn": turn, "halfw": half_in,
+        "turn": turn,
         "al1out": lambda: every(lambda k, h: left_out(k, h, 1), False),
     }
     steps = {
-        "lS": l_side_out, "lO": l_own, "lP": l_partner, "lL": l_last, "lZ": l_done,
+        "lS": l_side_out, "lR": l_pass, "lO": l_own, "lP": l_partner, "lB": l_own_rest,
+        "lL": l_last, "lZ": l_done,
         "lG": lambda t: l_far(t, 0), "lH": lambda t: l_far(t, 1),
         "rS": r_side_out, "rO": r_own, "rP": r_partner, "rZ": r_done,
         "rG": lambda t: r_far(t, 0), "rH": lambda t: r_far(t, 1),
@@ -458,7 +483,6 @@
 
     for c in sends:
         c.wait_send()
-    half_out.wait_send()
     every(lambda k, h: left_out(k, h, 0), True)
     every(right_out, True)
     every(lambda k, h: left_out(k, h, 1), True)
@@ -488,12 +512,13 @@
             pltpu.VMEM((512, 128), F32),
             pltpu.VMEM((8, 2, 144, 128), BF16),
             pltpu.VMEM((8, 2, 144, 128), BF16),
-            pltpu.VMEM((8, 2, 144, 128), BF16),
+            pltpu.VMEM((2, 4, 2, 144, 128), BF16),
             pltpu.VMEM((8, 2, 144, 128), BF16),
             pltpu.VMEM((2, 16, 8, 128, 128), BF16),
-            pltpu.VMEM((8, 128, 128), BF16),
+            pltpu.VMEM((2, 4, 128, 128), BF16),
+            pltpu.VMEM((16, 4, 16, 128), BF16),
+            pltpu.VMEM((4, 16, 128), BF16),
             pltpu.VMEM((8, 66, 32, 128), BF16),
-            pltpu.VMEM((64, 16, 128), BF16),
             pltpu.VMEM((2048, 128), F32),
             pltpu.VMEM((128, 1024), BF16),
             pltpu.VMEM((64, 256), BF16),
@@ -509,8 +534,8 @@
             pltpu.VMEM((1024, 128), BF16),
             pltpu.VMEM((2, 128), F32),
             dma((8,)), dma((9,)),
-            dma((3, 8, 2)), dma((2, 8, 2)), dma((8, 2)), dma(()), dma(()),
-            dma((Q + 1, 17)), dma((Q + 1, 17)), dma((Q, 9)), dma((Q, 9)),
+            dma((3, 8, 2)), dma((2, 2, 4, 2)), dma((8, 2)),
+            dma((Q + 1, 22)), dma((Q + 1, 22)), dma((P, 9)), dma((P, 9)),
         ],
         compiler_params=pltpu.CompilerParams(
             collective_id=0, has_side_effects=True, vmem_limit_bytes=61 << 20
@@ -528,17 +553,17 @@
         per_device,
         mesh=mesh,
         in_specs=(
-            P(("row", "col"), None, None),
-            P(("row", "col"), None),
-            P(),
-            P("row", "col", None),
-            P(),
-            P(),
-            P(),
-            P(),
-            P(),
-            P(),
+            Spec(("row", "col"), None, None),
+            Spec(("row", "col"), None),
+            Spec(),
+            Spec("row", "col", None),
+            Spec(),
+            Spec(),
+            Spec(),
+            Spec(),
+            Spec(),
+            Spec(),
         ),
-        out_specs=P("row", "col", None),
+        out_specs=Spec("row", "col", None),
         check_vma=False,
     )

time: 87.1 us -> 78.5 us (0.901)
  Pallas kernels: 85.6 us -> 76.2 us
    pallas_call x1, Pallas kernels: 85.6 us -> 76.2 us  [per_device(): pl.pallas_call(kernel, out_shape=pltpu.VMEM(pair_state.shape, BF16), in_s...]
where the time goes in v4:
time: 78.5 us; the launch traced here: 77.6 us
  Pallas kernels  76.2 us (97%)
  local copies, waits for them, and re-layouts  1.32 us (2%)
    pallas_call x1, Pallas kernels, per_device(): pl.pallas_call(kernel, out_shape=pltpu.VMEM(pair_state.shape, BF16), in_s...  76.2 us

profile of v4, /device:TPU:1, one launch (start us, length us, event | category | flops | bytes accessed | tf_op | source)
XLA Modules:
  0.0 77.6 jit_solution(10948329202262833727)
XLA Ops:
  0.0 76.2 %shard_map.100 = bf16[128,64,128]{2,1,0:T(8,128)(2,1)S(1)} custom-call(bf16[8,1024,256]{2,1,0:T(8,128)(2,1)} %feats.1, s32[8,1024]{1,0:T(8,128)} %flags_h.1, s32[8,128]{1,0:T(8,128)} %bitcast.7, bf16[128,64,128]{2,1,0:T(8,128)(2,1)} %pair.1, f32[1,256]{1,0:T(1,128)} %bitcast.8, f32[1,256]{1,0:T(1,128)} %bitcast.9, bf16[32,256]{1,0:T(8,128)(2,1)} %bitcast.5, ...), custom_call_target="tpu_custom_call" | custom-call | tf_op jit(solution)/shard_map/pallas_call | solution.py:505
  76.2 1.3 %copy.12 = bf16[128,64,128]{2,1,0:T(8,128)(2,1)} copy(bf16[128,64,128]{2,1,0:T(8,128)(2,1)S(1)} %shard_map.100) | data formatting | bytes 4194304

commit v5 on v4

--- a/solution.py
+++ b/solution.py
@@ -84,7 +84,7 @@
     for c in loads[:5]:
         c.wait()
 
-    def project(k, _):
+    def project(k):
         f_copy(k).wait()
         b = block_of(k)
         present = flags[:, pl.ds(pl.multiple_of(b * 128, 128), 128)].astype(F32)
@@ -117,9 +117,6 @@
         both = jnp.concatenate([present, jnp.zeros_like(present)], axis=0)
         SR[b, 0, 128:144, :] = pad
         SR[b, 1, 128:144, :] = pltpu.roll(both, 64, 1).astype(BF16)
-        return 0
-
-    lax.fori_loop(0, 8, project, 0)
 
     def left_part(part):
         return slice(0, PART) if part == 0 else slice(PART, 144)
@@ -140,24 +137,32 @@
         )
         return c, jnp.logical_and(b == cc, h == core)
 
+    def each(make, k, wait):
+        for h in range(2):
+            c, mine = make(k, h)
+
+            @pl.when(jnp.logical_not(mine))
+            def _():
+                c.wait_send() if wait else c.start()
+
     def every(make, wait):
-        def one(k, _):
-            for h in range(2):
-                c, mine = make(k, h)
-
-                @pl.when(jnp.logical_not(mine))
-                def _():
-                    c.wait_send() if wait else c.start()
-
-            return 0
-
-        lax.fori_loop(0, 8, one, 0)
-
+        lax.fori_loop(0, 8, lambda k, _: (each(make, k, wait), 0)[1], 0)
+
+    def send_block(k):
+        each(lambda k, h: left_out(k, h, 0), k, False)
+        each(right_out, k, False)
+
+    def project_and_send(k, _):
+        project(k)
+        send_block(k)
+        return 0
+
+    project(0)
     pl.semaphore_wait(bar, len(greeted))
+    send_block(0)
+    lax.fori_loop(1, 8, project_and_send, 0)
 
     def start():
-        every(lambda k, h: left_out(k, h, 0), False)
-        every(right_out, False)
         for i in range(2):
             RL[i, x, core] = SL[i * 4 + x, core]
         RR[cc, core] = SR[cc, core]

time: 78.5 us -> 77 us (0.981)
  Pallas kernels: 76.2 us -> 74.8 us
    pallas_call x1, Pallas kernels: 76.2 us -> 74.8 us  [per_device(): pl.pallas_call(kernel, out_shape=pltpu.VMEM(pair_state.shape, BF16), in_s...]
where the time goes in v5:
time: 77 us; the launch traced here: 76.1 us
  Pallas kernels  74.8 us (97%)
  local copies, waits for them, and re-layouts  1.32 us (2%)
    pallas_call x1, Pallas kernels, per_device(): pl.pallas_call(kernel, out_shape=pltpu.VMEM(pair_state.shape, BF16), in_s...  74.8 us

profile of v5, /device:TPU:1, one launch (start us, length us, event | category | flops | bytes accessed | tf_op | source)
XLA Modules:
  0.0 76.1 jit_solution(566956687478639934)
XLA Ops:
  0.0 74.8 %shard_map.100 = bf16[128,64,128]{2,1,0:T(8,128)(2,1)S(1)} custom-call(bf16[8,1024,256]{2,1,0:T(8,128)(2,1)} %feats.1, s32[8,1024]{1,0:T(8,128)} %flags_h.1, s32[8,128]{1,0:T(8,128)} %bitcast.7, bf16[128,64,128]{2,1,0:T(8,128)(2,1)} %pair.1, f32[1,256]{1,0:T(1,128)} %bitcast.8, f32[1,256]{1,0:T(1,128)} %bitcast.9, bf16[32,256]{1,0:T(8,128)(2,1)} %bitcast.5, ...), custom_call_target="tpu_custom_call" | custom-call | tf_op jit(solution)/shard_map/pallas_call | solution.py:510
  74.8 1.3 %copy.12 = bf16[128,64,128]{2,1,0:T(8,128)(2,1)} copy(bf16[128,64,128]{2,1,0:T(8,128)(2,1)S(1)} %shard_map.100) | data formatting | bytes 4194304

commit v6 on v5

--- a/solution.py
+++ b/solution.py
@@ -8,19 +8,18 @@
 MESH = pl.DeviceIdType.MESH
 F32 = jnp.float32
 BF16 = jnp.bfloat16
-LEFT = ((0, 2), (2, 2), (4, 2), (6, 1), (7, 1))
-RIGHT = ((0, 16), (16, 16), (32, 16), (48, 8), (56, 8))
+LEFT = ((0, 2), (2, 2), (4, 2), (6, 2))
+RIGHT = ((0, 16), (16, 16), (32, 16), (48, 16))
 ORDER = (
-    "start", "prep", "al1out", "join0", "lO0", "lS0", "turn", "rO0", "lR0", "lP0", "rS0", "rO1",
-    "join1", "lS1", "lO2", "lB0", "lH0", "lO1", "rG0", "rS1", "rP0", "lR1", "lG0", "lS2", "rG1",
-    "rS2", "lP1", "lO3", "rP1", "rO2", "lR2", "lL0", "lB1", "rH0", "lP2", "lZ0", "lH1", "rP2",
-    "rH1", "lG1", "lB2", "rG2", "rS3", "lH2", "lS4", "lS3", "rZ0", "u0.2.0.16", "rP3", "lL1",
-    "rS4", "rH2", "lR4", "rO4", "rO3", "lP4", "lR3", "lG2", "lP3", "lO4", "rZ1", "u0.2.16.16",
-    "lZ1", "u2.2.0.16", "rP4", "lB4", "u2.2.16.16", "lL2", "rH3", "lB3", "lH4", "rZ2",
-    "u0.2.32.16", "lH3", "u2.2.32.16", "rG4", "lG4", "rG3", "lZ2", "u4.2.16.16", "lG3", "rH4",
-    "u4.2.32.16", "u4.2.0.16", "lL4", "rZ3", "lL3", "rZ4", "u4.2.48.16", "u2.2.48.16", "lZ4",
-    "u0.2.48.16", "lZ3", "u6.2.16.16", "f1", "u6.2.0.16", "f0", "u6.2.48.16", "f3",
-    "u6.2.32.16", "f2",
+    "start", "prep", "al1out", "join0", "lS0", "lO0", "turn", "rS0", "rO0", "lR0", "lP0",
+    "join1", "lO1", "lS1", "rO2", "lH0", "rP0", "rG0", "rS1", "lB0", "lR1", "rG2", "lP1", "lG0",
+    "rP1", "rH0", "rO1", "rS2", "lB1", "lH1", "lS2", "lO2", "lL0", "rP2", "lG1", "rH1", "lR2",
+    "lP2", "lS3", "lZ0", "rZ0", "u0.2.0.16", "lL1", "rG1", "rS3", "lB2", "lR3", "lP3", "lH2",
+    "rH2", "rO3", "lZ1", "u2.2.0.16", "lG2", "lO3", "rP3", "rZ1", "u2.2.16.16", "lB3", "lH3",
+    "rZ2", "u0.2.32.16", "u2.2.32.16", "lL2", "u0.2.16.16", "rG3", "lG3", "rH3", "lZ2",
+    "u4.2.32.16", "u4.2.16.16", "u4.2.0.16", "rZ3", "lL3", "u0.2.48.16", "u2.2.48.16",
+    "u4.2.48.16", "lZ3", "u6.2.32.16", "u6.2.0.16", "f0", "f2", "u6.2.48.16", "f3",
+    "u6.2.16.16", "f1",
 )
 Q, P = len(LEFT), len(RIGHT)
 MQ = 1

time: 77 us -> 77.2 us (level)
  Pallas kernels: 74.8 us -> 75.7 us
    pallas_call x1, Pallas kernels: 74.8 us -> 75.7 us  [per_device(): pl.pallas_call(kernel, out_shape=pltpu.VMEM(pair_state.shape, BF16), in_s...]
where the time goes in v6:
time: 77.2 us; the launch traced here: 77.1 us
  Pallas kernels  75.7 us (98%)
  local copies, waits for them, and re-layouts  1.32 us (2%)
    pallas_call x1, Pallas kernels, per_device(): pl.pallas_call(kernel, out_shape=pltpu.VMEM(pair_state.shape, BF16), in_s...  75.7 us

profile of v6, /device:TPU:1, one launch (start us, length us, event | category | flops | bytes accessed | tf_op | source)
XLA Modules:
  0.0 77.1 jit_solution(13659796103431283245)
XLA Ops:
  0.0 75.7 %shard_map.100 = bf16[128,64,128]{2,1,0:T(8,128)(2,1)S(1)} custom-call(bf16[8,1024,256]{2,1,0:T(8,128)(2,1)} %feats.1, s32[8,1024]{1,0:T(8,128)} %flags_h.1, s32[8,128]{1,0:T(8,128)} %bitcast.7, bf16[128,64,128]{2,1,0:T(8,128)(2,1)} %pair.1, f32[1,256]{1,0:T(1,128)} %bitcast.8, f32[1,256]{1,0:T(1,128)} %bitcast.9, bf16[32,256]{1,0:T(8,128)(2,1)} %bitcast.5, ...), custom_call_target="tpu_custom_call" | custom-call | tf_op jit(solution)/shard_map/pallas_call | solution.py:509
  75.7 1.3 %copy.12 = bf16[128,64,128]{2,1,0:T(8,128)(2,1)} copy(bf16[128,64,128]{2,1,0:T(8,128)(2,1)S(1)} %shard_map.100) | data formatting | bytes 4194304
